TPU v7x, 32 devices: a whole 2x2x4 slice. The times are simulated.
32 devices in a mesh: grp: 2 (over core), seq: 4 (over y, x), head: 4 (over z).
Axes of the slice: x: 2, y: 2, z: 4, core: 2. Of those that a mesh axis runs over, the one named last changes fastest.
Arguments:
- queries: bfloat16 [1024, 2048], P(('grp', 'seq'), 'head'), may hold values from -100 to 100
- keys: bfloat16 [2, 4096, 2048], P(None, ('grp', 'seq'), 'head'), may hold values from -15 to 15
- values: bfloat16 [2, 4096, 2048], P(None, ('grp', 'seq'), 'head'), may hold values from -6 to 6
- grad_out: bfloat16 [1024, 2048], P(('grp', 'seq', 'head')), may hold values from -6 to 6
- pad_counts: int32 [2], replicated, may hold values from 0 to 256, as said below
Outputs:
- context: bfloat16 [1024, 2048], P(('grp', 'seq', 'head'))
- grad_queries: bfloat16 [1024, 2048], P(('grp', 'seq'), 'head')
- grad_keys: bfloat16 [2, 4096, 2048], P(None, ('grp', 'seq'), 'head')
- grad_values: bfloat16 [2, 4096, 2048], P(None, ('grp', 'seq'), 'head')
Inputs may be any that keep to these rules, and one draw needn't show every extreme that they name: `pad_counts`: each count is at most 256, and in every draw one pair has exactly 256 padding tokens.
All inputs are finite; a program needn't handle non-finite values.
Results may differ from a plain program's by a relative error of at most 0.0215.
Values may be sent and summed in bfloat16 or wider, within the bound.
No kernel may reach another device: no remote copies, remote signals or barrier semaphores. Data moves between devices by JAX's collectives and lax.ppermute only.
A program may use at most 64 MiB of HBM per device.

v0:
```python
import math

import jax
import jax.numpy as jnp
from jax import lax
from jax.sharding import PartitionSpec as P

HEAD_DIM = 64


def valid_rows(pad_counts, first, rows, seq_len):
    position = first + jnp.arange(rows, dtype=jnp.int32)
    which = position // seq_len
    within = position % seq_len
    onehot = which[:, None] == jnp.arange(pad_counts.shape[0], dtype=jnp.int32)[None, :]
    pads = jnp.sum(jnp.where(onehot, pad_counts[None, :], 0), axis=1)
    return (within < seq_len - pads).astype(jnp.float32)


def source_blocks(array, heads_here):
    batch, rows, width = array.shape
    block = math.gcd(rows, 128)
    return array.reshape(batch, rows // block, block, heads_here, HEAD_DIM).transpose(1, 0, 2, 3, 4)


def pair_scores(query_heads, key_block, scale):
    return (
        jnp.einsum("bthd,bphd->bhtp", query_heads, key_block, preferred_element_type=jnp.float32)
        * scale
    )


def local(queries, keys, values, grad_out, pad_counts):
    rows, width = queries.shape
    heads_here = width // HEAD_DIM
    batch = keys.shape[0]
    scale = 1.0 / math.sqrt(HEAD_DIM)
    group = lax.axis_size(("grp", "seq"))
    seq_len = rows * group // batch
    first = lax.axis_index(("grp", "seq")) * rows
    valid = valid_rows(pad_counts, first, rows, seq_len)
    grad_cols = lax.all_to_all(grad_out, "head", split_axis=1, concat_axis=0, tiled=True)
    masked_mine = jnp.where(valid[:, None] > 0, grad_cols, jnp.zeros((), jnp.bfloat16))
    query_all, grad_all = (
        lax.all_gather(queries, ("grp", "seq"), axis=0, tiled=True),
        lax.all_gather(masked_mine, ("grp", "seq"), axis=0, tiled=True),
    )
    query_heads = query_all.reshape(batch, seq_len, heads_here, HEAD_DIM)
    grad_heads = grad_all.reshape(batch, seq_len, heads_here, HEAD_DIM)
    key_blocks = source_blocks(keys, heads_here)
    value_blocks = source_blocks(values, heads_here)

    def stats_step(state, key_block):
        top, total = state
        scores = pair_scores(query_heads, key_block, scale)
        new_top = jnp.maximum(top, jnp.max(scores, axis=-1))
        total = total * jnp.exp(top - new_top) + jnp.sum(
            jnp.exp(scores - new_top[..., None]), axis=-1
        )
        return ((new_top, total), None)

    start = (
        jnp.full((batch, heads_here, seq_len), -1e30, jnp.float32),
        jnp.zeros((batch, heads_here, seq_len), jnp.float32),
    )
    (top, total), unused = lax.scan(stats_step, start, key_blocks)
    row_top = lax.pmax(top, ("grp", "seq"))
    row_total = lax.psum(total * jnp.exp(top - row_top), ("grp", "seq"))

    def forward_step(accum, item):
        key_block, value_block = item
        scores = pair_scores(query_heads, key_block, scale)
        probs = jnp.exp(scores - row_top[..., None]) / row_total[..., None]
        added = jnp.einsum(
            "bhtp,bphd->bthd",
            probs.astype(jnp.bfloat16),
            value_block,
            preferred_element_type=jnp.float32,
        )
        return (accum + added, None)

    partial_value, unused = lax.scan(
        forward_step,
        jnp.zeros((batch, seq_len, heads_here, HEAD_DIM), jnp.float32),
        (key_blocks, value_blocks),
    )
    partial_value = partial_value.reshape(batch * seq_len, width)
    summed = lax.psum(partial_value, ("grp", "seq"))
    attended = lax.dynamic_slice_in_dim(summed, first, rows, 0) * valid[:, None]
    delta_rows = jnp.sum(
        (grad_all.astype(jnp.float32) * summed).reshape(batch * seq_len, heads_here, HEAD_DIM),
        axis=-1,
    )
    delta = delta_rows.reshape(batch, seq_len, heads_here).transpose(0, 2, 1)
    context = lax.all_to_all(
        attended.astype(jnp.bfloat16), "head", split_axis=0, concat_axis=1, tiled=True
    )

    def backward_step(grad_q, item):
        key_block, value_block = item
        scores = pair_scores(query_heads, key_block, scale)
        probs = jnp.exp(scores - row_top[..., None]) / row_total[..., None]
        weights = probs.astype(jnp.bfloat16)
        grad_probs = jnp.einsum(
            "bthd,bphd->bhtp", grad_heads, value_block, preferred_element_type=jnp.float32
        )
        grad_scores = (probs * (grad_probs - delta[..., None]) * scale).astype(jnp.bfloat16)
        grad_q = grad_q + jnp.einsum(
            "bhtp,bphd->bthd", grad_scores, key_block, preferred_element_type=jnp.float32
        )
        grad_k = jnp.einsum(
            "bhtp,bthd->bphd", grad_scores, query_heads, preferred_element_type=jnp.float32
        )
        grad_v = jnp.einsum(
            "bhtp,bthd->bphd", weights, grad_heads, preferred_element_type=jnp.float32
        )
        return (grad_q, (grad_k.astype(jnp.bfloat16), grad_v.astype(jnp.bfloat16)))

    grad_q, (key_parts, value_parts) = lax.scan(
        backward_step,
        jnp.zeros((batch, seq_len, heads_here, HEAD_DIM), jnp.float32),
        (key_blocks, value_blocks),
    )
    src_rows = keys.shape[1]
    grad_keys = key_parts.transpose(1, 0, 2, 3, 4).reshape(batch, src_rows, width)
    grad_values = value_parts.transpose(1, 0, 2, 3, 4).reshape(batch, src_rows, width)
    grad_queries = lax.psum_scatter(
        grad_q.reshape(batch * seq_len, width), ("grp", "seq"), scatter_dimension=0, tiled=True
    )
    return (context, grad_queries.astype(jnp.bfloat16), grad_keys, grad_values)


def solution(mesh):
    return jax.shard_map(
        local,
        mesh=mesh,
        in_specs=(
            P(("grp", "seq"), "head"),
            P(None, ("grp", "seq"), "head"),
            P(None, ("grp", "seq"), "head"),
            P(("grp", "seq", "head"), None),
            P(),
        ),
        out_specs=(
            P(("grp", "seq", "head"), None),
            P(("grp", "seq"), "head"),
            P(None, ("grp", "seq"), "head"),
            P(None, ("grp", "seq"), "head"),
        ),
        check_vma=False,
    )
```

profile of v0, /device:TPU:0, one launch (start us, length us, event | category | flops | bytes accessed | tf_op | source)
XLA Modules:
  0.0 273.2 jit_solution(14110220472855164641)
XLA Ops:
  7.9 1.6 copy.115
  9.5 6.3 %all-to-all-start.1 = ((bf16[32,4,512]{2,0,1:T(8,128)(2,1)}), bf16[32,4,512]{2,0,1:T(8,128)(2,1)S(1)}, u32[]{:S(2)}, u32[]{:S(2)}) async-start(bf16[32,4,512]{2,0,1:T(8,128)(2,1)} %bitcast.90), calls=%async_computation.1 | async-start | bytes 262144 | tf_op jit(solution)/shard_map/all_to_all | solution.py:42
  15.8 1.5 copy.82
  17.9 1.5 copy.81
  20.1 1.7 all-to-all-done.1
  22.7 13.4 %all-gather.3.cloned.1.call-done = bf16[1024,512]{1,0:T(8,128)(2,1)} async-done(((bf16[128,512]{1,0:T(8,128)(2,1)}), bf16[1024,512]{1,0:T(8,128)(2,1)}) %all-gather.3.cloned.1.call-update) | async-done | bytes 1048592 | tf_op jit(solution)/shard_map/all_gather | solution.py:45
  36.1 3.9 %reshape.106 = bf16[2,512,8,64]{3,2,1,0:T(8,128)(2,1)} reshape(bf16[1024,512]{1,0:T(8,128)(2,1)} %all-gather.3.cloned.1.call-done) | data formatting | bytes 2097152 | tf_op jit(solution)/shard_map/reshape | solution.py:48
  40.0 2.5 copy.88
  42.5 6.5 %while.39 = (s32[]{:T(128)}, f32[2,8,512]{2,1,0:T(8,128)S(1)}, f32[2,8,512]{2,1,0:T(8,128)S(1)}, bf16[4,2,128,8,64]{2,4,3,1,0:T(8,128)(2,1)S(1)}, bf16[2,512,8,64]{1,3,2,0:T(8,128)(2,1)S(1)}, /*index=5*/s32[]{:T(128)}, s32[]{:T(128)}) while((s32[]{:T(128)}, f32[2,8,512]{2,1,0:T(8,128)S(1)}, f32[2,8,512]{2,1,0:T(8,128)S(1)}, ...), condition=%wide.region_3.4_spmd.clone, body=%wide.region_0.3_spmd.clone.sunk | while | flops 139501568 | bytes 10125412 | solution.py:66
  49.0 26.6 %pmax.7 = f32[2,8,512]{2,1,0:T(8,128)S(1)} all-reduce(f32[2,8,512]{2,1,0:T(8,128)S(1)} %get-tuple-element.128), channel_id=1, replica_groups=mesh['grp'=2,'seq'=4,'head'=4] {'grp','seq'}, use_global_device_ids=true, to_apply=%region_4.5 | all-reduce | flops 8192 | bytes 65536 | tf_op jit(solution)/shard_map/pmax | solution.py:67
  75.6 26.0 %psum.14 = f32[2,8,512]{2,1,0:T(8,128)S(1)} all-reduce(f32[2,8,512]{2,1,0:T(8,128)S(1)} %exponential_multiply_fusion), channel_id=1, replica_groups=mesh['grp'=2,'seq'=4,'head'=4] {'grp','seq'}, use_global_device_ids=true, to_apply=%region_5.6 | all-reduce | flops 8192 | bytes 65536 | tf_op jit(solution)/shard_map/psum | solution.py:68
  101.6 15.5 %while.40 = (s32[]{:T(128)}, f32[2,512,8,64]{1,3,2,0:T(8,128)}, bf16[4,2,128,8,64]{2,4,3,1,0:T(8,128)(2,1)S(1)}, bf16[4,2,128,8,64]{2,4,3,1,0:T(8,128)(2,1)S(1)}...) while((s32[]{:T(128)}, f32[2,512,8,64]{1,3,2,0:T(8,128)}, ...), condition=%wide.region_7.8_spmd.clone, body=%wide.region_6.7_spmd.clone.sunk | while | flops 273678336 | bytes 5834350 | solution.py:82
  101.6 2.7 bitcast_add_fusion.4
  104.3 4.3 %bitcast_add_fusion.4 = f32[2,512,8,64]{1,3,2,0:T(8,128)} fusion(f32[2,512,8,64]{1,3,2,0:T(8,128)} %get-tuple-element.553, bf16[2,512,8,64]{1,3,2,0:T(8,128)(2,1)S(1)} %get-tuple-element.565, f32[2,8,512]{2,1,0:T(8,128)S(1)} %get-tuple-element.567, f32[2,8,512]{2,1,0:T(8,128)S(1)} %get-tuple-element.566, pred[]{:T(512)S(6)} %compare.23, ...), kind=kOutput, calls=%fused_computation.12.clone.1 | convolution fusion | flops 273678336 | bytes 5834240 | tf_op jit(solution)/shard_map/while/body/eval_jaxpr/bhtp,bphd->bthd/dot_general | solution.py:74
  108.5 4.3 %bitcast_add_fusion.4 = f32[2,512,8,64]{1,3,2,0:T(8,128)} fusion(f32[2,512,8,64]{1,3,2,0:T(8,128)} %get-tuple-element.553, bf16[2,512,8,64]{1,3,2,0:T(8,128)(2,1)S(1)} %get-tuple-element.565, f32[2,8,512]{2,1,0:T(8,128)S(1)} %get-tuple-element.567, f32[2,8,512]{2,1,0:T(8,128)S(1)} %get-tuple-element.566, pred[]{:T(512)S(6)} %compare.23, ...), kind=kOutput, calls=%fused_computation.12.clone.1 | convolution fusion | flops 273678336 | bytes 5834240 | tf_op jit(solution)/shard_map/while/body/eval_jaxpr/bhtp,bphd->bthd/dot_general | solution.py:74
  112.8 4.3 %bitcast_add_fusion.4 = f32[2,512,8,64]{1,3,2,0:T(8,128)} fusion(f32[2,512,8,64]{1,3,2,0:T(8,128)} %get-tuple-element.553, bf16[2,512,8,64]{1,3,2,0:T(8,128)(2,1)S(1)} %get-tuple-element.565, f32[2,8,512]{2,1,0:T(8,128)S(1)} %get-tuple-element.567, f32[2,8,512]{2,1,0:T(8,128)S(1)} %get-tuple-element.566, pred[]{:T(512)S(6)} %compare.23, ...), kind=kOutput, calls=%fused_computation.12.clone.1 | convolution fusion | flops 273678336 | bytes 5834240 | tf_op jit(solution)/shard_map/while/body/eval_jaxpr/bhtp,bphd->bthd/dot_general | solution.py:74
  117.1 3.6 %copy.89 = f32[2,512,8,64]{1,0,3,2:T(2,128)S(1)} copy(f32[2,512,8,64]{1,3,2,0:T(8,128)} %get-tuple-element.130) | data formatting | bytes 4194304 | tf_op jit(solution)/shard_map/while | solution.py:82
  120.7 1.8 copy.112
  122.8 2.7 reshape.98
  125.4 1.4 copy.97
  126.9 58.4 %all-reduce.2.cloned.1.call-done = f32[1024,512]{0,1:T(8,128)} async-done(((f32[1024,512]{0,1:T(8,128)}), f32[1024,512]{0,1:T(8,128)}) %all-reduce.2.cloned.1.call-update) | async-done | bytes 2097168 | tf_op jit(solution)/shard_map/psum | solution.py:88
  185.3 2.2 bitcast_reduce_fusion.1
  187.5 31.9 %while.41 = (s32[]{:T(128)}, f32[2,512,8,64]{1,3,2,0:T(8,128)}, bf16[4,2,128,8,64]{2,4,3,1,0:T(8,128)(2,1)}, bf16[4,2,128,8,64]{2,4,3,1,0:T(8,128)(2,1)}, bf16[4...) while((s32[]{:T(128)}, f32[2,512,8,64]{1,3,2,0:T(8,128)}, ...), condition=%wide.region_12.13_spmd.clone, body=%wide.region_11.12_spmd.clone.sunk | while | flops 680787968 | bytes 45449432 | solution.py:119
  188.5 1.6 fusion.83
  190.1 1.8 multiply_convert_fusion.3
  191.9 1.6 fusion.82
  194.2 1.3 copy-done.1
  196.5 1.6 fusion.83
  198.1 1.8 multiply_convert_fusion.3
  199.8 1.6 fusion.82
  202.1 1.3 copy-done.1
  204.5 1.6 fusion.83
  206.0 1.8 multiply_convert_fusion.3
  207.8 1.6 fusion.82
  210.1 1.3 copy-done.1
  212.4 1.6 fusion.83
  214.0 1.8 multiply_convert_fusion.3
  215.8 1.6 fusion.82
  218.1 1.3 copy-done.1
  219.4 3.2 %copy.98 = f32[2,512,8,64]{1,0,3,2:T(2,128)S(1)} copy(f32[2,512,8,64]{1,3,2,0:T(8,128)} %get-tuple-element.131) | data formatting | bytes 4194304 | tf_op jit(solution)/shard_map/while | solution.py:119
  222.6 1.8 copy.113
  224.4 1.1 multiply_convert_fusion.1
  226.2 4.6 %all-to-all-start = ((bf16[4,32,512]{2,1,0:T(8,128)(2,1)}), bf16[4,32,512]{2,1,0:T(8,128)(2,1)S(1)}, u32[]{:S(2)}, u32[]{:S(2)}) async-start(bf16[4,32,512]{2,1,0:T(8,128)(2,1)} %bitcast.2), calls=%async_computation | async-start | bytes 262144 | tf_op jit(solution)/shard_map/all_to_all | solution.py:95
  230.8 1.2 copy.105
  232.0 2.1 reshape.105
  234.1 1.2 copy.104
  235.2 2.0 reshape.104
  237.9 27.0 %reduce-scatter.2.cloned.1.call-done = f32[128,512]{0,1:T(8,128)} async-done(((f32[1024,512]{0,1:T(8,128)}), f32[128,512]{0,1:T(8,128)}) %reduce-scatter.2.cloned.1.call-update) | async-done | bytes 262160 | tf_op jit(solution)/shard_map/reduce_scatter | solution.py:127
  (78 shorter events, 19.5 us)
Async XLA Ops:
  7.2 28.9 %all-gather.3.cloned.1.call-start = ((), (), s32[]{:S(2)}) async-start(), calls=%async_computation.3 | async-start | bytes 1179648 | tf_op jit(solution)/shard_map/all_gather | solution.py:45
  9.5 12.4 %all-to-all-start.1 = ((bf16[32,4,512]{2,0,1:T(8,128)(2,1)}), bf16[32,4,512]{2,0,1:T(8,128)(2,1)S(1)}, u32[]{:S(2)}, u32[]{:S(2)}) async-start(bf16[32,4,512]{2,0,1:T(8,128)(2,1)} %bitcast.90), calls=%async_computation.1 | async-start | bytes 262144 | tf_op jit(solution)/shard_map/all_to_all | solution.py:42
  15.8 107.0 %all-gather.5.cloned.1.call-start = ((), (), s32[]{:S(2)}) async-start(), calls=%async_computation.5 | async-start | bytes 1179648 | tf_op jit(solution)/shard_map/all_gather | solution.py:46
  19.4 0.7 copy-start.5
  22.7 162.6 %all-reduce.2.cloned.1.call-start = ((), (), s32[]{:S(2)}) async-start(), calls=%async_computation.4 | async-start | bytes 4194304 | tf_op jit(solution)/shard_map/psum | solution.py:88
  117.1 3.6 %copy-start.2 = (bf16[4,2,128,8,64]{2,4,3,1,0:T(8,128)(2,1)}, bf16[4,2,128,8,64]{2,4,3,1,0:T(8,128)(2,1)S(1)}, u32[]{:S(2)}) copy-start(bf16[4,2,128,8,64]{2,4,3,1,0:T(8,128)(2,1)S(1)} %get-tuple-element.621) | copy-start | bytes 3145732
  122.5 142.4 %reduce-scatter.2.cloned.1.call-start = ((), (), s32[]{:S(2)}) async-start(), calls=%async_computation.6 | async-start | bytes 2359296 | tf_op jit(solution)/shard_map/reduce_scatter | solution.py:127
  191.9 1.6 copy-start
  194.2 1.3 copy-start.1
  199.8 1.6 copy-start
  202.1 1.3 copy-start.1
  207.8 1.6 copy-start
  210.1 1.3 copy-start.1
  215.8 1.6 copy-start
  218.1 1.3 copy-start.1
  224.3 6.5 %copy-start.3 = (bf16[4,2,128,8,64]{2,4,3,1,0:T(8,128)(2,1)S(1)}, bf16[4,2,128,8,64]{2,4,3,1,0:T(8,128)(2,1)}, u32[]{:S(2)}) copy-start(bf16[4,2,128,8,64]{2,4,3,1,0:T(8,128)(2,1)} %get-tuple-element.133) | copy-start | bytes 3145732
  226.2 11.1 %all-to-all-start = ((bf16[4,32,512]{2,1,0:T(8,128)(2,1)}), bf16[4,32,512]{2,1,0:T(8,128)(2,1)S(1)}, u32[]{:S(2)}, u32[]{:S(2)}) async-start(bf16[4,32,512]{2,1,0:T(8,128)(2,1)} %bitcast.2), calls=%async_computation | async-start | bytes 262144 | tf_op jit(solution)/shard_map/all_to_all | solution.py:95
  232.0 2.1 copy-start.4
Sparse Core Ops, SparseCore 0:
  9.9 26.1 all-gather.2
  38.6 23.6 all-gather.4
  122.6 62.6 all-reduce.1
  224.5 40.3 reduce-scatter.1
where the time goes:
time: 274 us; the launch traced here: 273 us
  waiting for transfers between devices  101 us (37%)
  blocking collectives  52.6 us (19%)
  matrix products  45 us (16%)
  local copies, waits for them, and re-layouts  40.6 us (15%)
  between operations  14 us (5%)
  starting transfers between devices  11.2 us (4%)
  other arithmetic  8.19 us (3%)
    psum x1, waiting for transfers between devices, local(): summed = lax.psum(partial_value, ('grp', 'seq'))  58.4 us
    reduce_scatter x1, waiting for transfers between devices, local(): lax.psum_scatter(grad_q.reshape(batch * seq_len, width), ('grp', 'seq'),...  27 us
    pmax x1, blocking collectives, local(): row_top = lax.pmax(top, ('grp', 'seq'))  26.6 us
    psum x1, blocking collectives, local(): row_total = lax.psum(total * jnp.exp(top - row_top), ('grp', 'seq'))  26 us
    unnamed x21, local copies, waits for them, and re-layouts  18.2 us
    dot_general x4, matrix products, forward_step(): jnp.einsum('bhtp,bphd->bthd', probs.astype(jnp.bfloat16), value_block, pr...  15.5 us
    all_gather x1, waiting for transfers between devices, local(): lax.all_gather(queries, ('grp', 'seq'), axis=0, tiled=True)  13.4 us
    dot_general x8, matrix products, pair_scores(): jnp.einsum('bthd,bphd->bhtp', query_heads, key_block, preferred_element_t...  7.21 us
  transfers between devices with their start and end apart: 6, of which 4 were waited for; matrix products, arithmetic and copies ran while one was open for 19% of the time, Pallas kernels for 0%

commit v1 on v0

v1 whole, which is shorter than its diff:
```python
import math

import jax
import jax.numpy as jnp
from jax import lax
from jax.experimental import pallas as pl
from jax.experimental.pallas import tpu as pltpu
from jax.sharding import PartitionSpec as P

HEAD_DIM = 64
PAIR = 128
LOG2E = math.log2(math.e)
F32 = jnp.float32
BF16 = jnp.bfloat16
VMEM_LIMIT = 28 * 1024 * 1024

NT = (((1,), (1,)), ((), ()))
NN = (((1,), (0,)), ((), ()))


def dot(a, b, dims):
    return lax.dot_general(a, b, dims, preferred_element_type=F32)


def lane_mask(head, value):
    lane = lax.broadcasted_iota(jnp.int32, (1, PAIR), 1)
    return jnp.where((lane // HEAD_DIM) == head, value, 0.0).astype(BF16)


def lane_scale():
    return jnp.full((1, PAIR), 1.0 / math.sqrt(HEAD_DIM), F32).astype(BF16)


def stack_slots(refs, slots, lanes):
    return jnp.concatenate([refs[k][:, lanes] for k in slots], axis=0)


def slot_valid(info, n, rows, k):
    valid = rows * n - info[2 + info[0]]
    return jnp.clip(valid - (info[1] ^ k) * rows, 0, rows)


def any_valid(info, n, rows, slots):
    return sum(slot_valid(info, n, rows, k) for k in slots) > 0


def target_blocks(n, rows):
    per = max(1, min(n, 256 // rows))
    return [list(range(first, min(first + per, n))) for first in range(0, n, per)]


def for_valid_blocks(n, rows, info, run):
    blocks = target_blocks(n, rows)
    some = [any_valid(info, n, rows, slots) for slots in blocks]
    for case in range(1, 1 << len(blocks)):
        chosen = [b for b in range(len(blocks)) if case >> b & 1]
        wanted = True
        for b in range(len(blocks)):
            wanted = jnp.logical_and(wanted, some[b] if b in chosen else jnp.logical_not(some[b]))

        @pl.when(wanted)
        def _(chosen=chosen):
            rest = [blocks[b] for b in range(len(blocks)) if b not in chosen]
            run([blocks[b] for b in chosen], rest)


def chunked(refs):
    rows = min(256, refs[0].shape[0])
    return [x[i * rows : (i + 1) * rows] for x in refs for i in range(x.shape[0] // rows)]


def head_rows(x, u):
    zero = jnp.zeros((HEAD_DIM, x.shape[1]), BF16)
    part = x[u * HEAD_DIM : (u + 1) * HEAD_DIM]
    return jnp.concatenate([part, zero] if u == 0 else [zero, part], axis=0)


def minus_rows(x):
    high = x.astype(BF16).astype(F32)
    mid = (x - high).astype(BF16).astype(F32)
    low = x - high - mid
    row = lax.broadcasted_iota(jnp.int32, (16, x.shape[1]), 0)
    top = jnp.where(row == 0, -high, jnp.where(row == 1, -mid, jnp.where(row == 2, -low, 0.0))).astype(BF16)
    return jnp.concatenate([top, jnp.zeros((PAIR - 16, x.shape[1]), BF16)], axis=0)


def with_ones(x):
    lane = lax.broadcasted_iota(jnp.int32, (x.shape[0], PAIR), 1)
    return jnp.concatenate([x, (lane < 3).astype(F32).astype(BF16)], axis=1)


def forward_kernel(n, rows, info, *refs):
    q = refs[:n]
    k_own, v_own, k_oth, v_oth, lse_ref, top_ref, out_ref, exp_ref = refs[n:]
    first_pair = pl.program_id(0) * lse_ref.shape[0]

    def run(blocks, rest):
        def sources(own, oth, lanes):
            return chunked([own[0, :, lanes], oth[0, :, lanes]])

        ks, vts, qts = {}, {}, {}
        for p in range(lse_ref.shape[0]):
            lanes = slice(p * PAIR, (p + 1) * PAIR)
            ks[p] = sources(k_own, k_oth, lanes)
            vt = [x.T for x in sources(v_own, v_oth, lanes)]
            row = lax.broadcasted_iota(jnp.int32, (16, vt[0].shape[1]), 0)
            ones = (row == 0).astype(F32).astype(BF16)
            for u in range(2):
                vts[p, u] = [jnp.concatenate([x[u * HEAD_DIM : (u + 1) * HEAD_DIM], ones], axis=0) for x in vt]
            for b, slots in enumerate(blocks):
                qts[p, b] = (stack_slots(q, slots, lanes) * lane_scale()).T

        def scores(chain):
            p, b, u = chain
            qm = head_rows(qts[p, b], u)
            s = [dot(k, qm, NN) for k in ks[p]]
            top = jnp.max(s[0], axis=0, keepdims=True)
            for x in s[1:]:
                top = jnp.maximum(top, jnp.max(x, axis=0, keepdims=True))
            return s, top

        def output(chain, s, top):
            p, b, u = chain
            o = None
            block = target_blocks(n, rows).index(blocks[b])
            for c, (x, v) in enumerate(zip(s, vts[p, u])):
                e = jnp.exp2((x - top) * LOG2E).astype(BF16)
                exp_ref[first_pair + p, 2 * block + u, c] = e
                part = dot(v, e, NN)
                o = part if o is None else o + part
            total = o[HEAD_DIM : HEAD_DIM + 1]
            cols = pl.ds(blocks[b][0] * rows, rows * len(blocks[b]))
            lse_ref[p, u : u + 1, cols] = top + jnp.log(total)
            top_ref[p, u : u + 1, cols] = top
            out_ref[p * PAIR + u * HEAD_DIM : p * PAIR + (u + 1) * HEAD_DIM, cols] = o[:HEAD_DIM] / total

        chains = [(p, b, u) for p in range(lse_ref.shape[0]) for b in range(len(blocks)) for u in range(2)]
        ahead = scores(chains[0])
        for i, chain in enumerate(chains):
            now = ahead
            if i + 1 < len(chains):
                ahead = scores(chains[i + 1])
            output(chain, *now)
        for slots in rest:
            width = rows * len(slots)
            cols = pl.ds(slots[0] * rows, width)
            lse_ref[:, :, cols] = jnp.zeros((lse_ref.shape[0], 2, width), F32)
            top_ref[:, :, cols] = jnp.zeros((lse_ref.shape[0], 2, width), F32)
            out_ref[:, cols] = jnp.zeros((out_ref.shape[0], width), F32)

    for_valid_blocks(n, rows, info, run)


def slot_cotangents(g, info, n, slots, cols=slice(None)):
    blocks = []
    for k in slots:
        block = g[k][:, cols]
        row = lax.broadcasted_iota(jnp.int32, block.shape, 0)
        blocks.append(block * (row < slot_valid(info, n, block.shape[0], k)).astype(F32).astype(BF16))
    return jnp.concatenate(blocks, axis=0)


def delta_kernel(n, rows, info, *refs):
    g, (lse_ref, out_ref, stats_ref), sends = refs[:n], refs[n : n + 3], refs[n + 3 :]
    pairs = lse_ref.shape[0]
    for h in range(pairs):
        do = slot_cotangents(g, info, n, range(n), slice(h * PAIR, (h + 1) * PAIR)).T.astype(F32)
        prod = do * out_ref[h * PAIR : (h + 1) * PAIR]
        stats_ref[h, 0:2] = lse_ref[h]
        for u in range(2):
            part = prod[u * HEAD_DIM : (u + 1) * HEAD_DIM]
            stats_ref[h, 2 + u : 3 + u] = jnp.sum(part, axis=0, keepdims=True)
    for k in range(n):
        sends[k][...] = out_ref[:, k * rows : (k + 1) * rows].astype(BF16)


def merge(lses, deltas):
    top = lses[0]
    for x in lses[1:]:
        top = jnp.maximum(top, x)
    weights = [jnp.exp(x - top) for x in lses]
    total = sum(weights)
    delta = sum(w * d for w, d in zip(weights, deltas)) / total
    return top + jnp.log(total), delta


def backward_kernel(n, rows, info, *refs):
    q, g, stats = refs[:n], refs[n : 2 * n], refs[2 * n : 3 * n]
    k_own, v_own, k_oth, v_oth, top_ref, exp_ref = refs[3 * n : 3 * n + 6]
    dk_own, dv_own, d_oth = refs[3 * n + 6 : 3 * n + 9]
    dq = refs[3 * n + 9 :]
    first_pair = pl.program_id(0) * top_ref.shape[0]
    scale = 1.0 / math.sqrt(HEAD_DIM)

    def ordered(j, p, kind, u, slots):
        line = stats[j][p, 2 * kind + u : 2 * kind + u + 1]
        if rows % 128:
            return line[:, slots[0] * rows : (slots[-1] + 1) * rows]
        return jnp.concatenate([line[:, (k ^ j) * rows : ((k ^ j) + 1) * rows] for k in slots], axis=1)

    def run(blocks, rest):
        def sources(own, oth, lanes):
            return chunked([own[0, :, lanes], oth[0, :, lanes]])

        vs, kt, operands = {}, {}, {}
        pairs = stats[0].shape[0]
        for p in range(pairs):
            lanes = slice(p * PAIR, (p + 1) * PAIR)
            vs[p] = [with_ones(x) for x in sources(v_own, v_oth, lanes)]
            kt[p] = [x.T for x in sources(k_own, k_oth, lanes)]
            for b, slots in enumerate(blocks):
                qb = stack_slots(q, slots, lanes) * lane_scale()
                gb = slot_cotangents(g, info, n, slots, lanes)
                gt = gb.T
                cols = slice(slots[0] * rows, (slots[-1] + 1) * rows)
                for u in range(2):
                    lse, delta = merge(
                        [ordered(j, p, 0, u, slots) for j in range(n)], [ordered(j, p, 1, u, slots) for j in range(n)]
                    )
                    operands[p, b, u] = (
                        jnp.exp(top_ref[p, u : u + 1, cols] - lse),
                        jnp.concatenate([head_rows(gt, u), minus_rows(delta)], axis=0),
                        qb * lane_mask(u, 1.0),
                        gb * lane_mask(u, 1.0),
                    )
        count, size = len(vs[0]), vs[0][0].shape[0]
        dks, dvs, dqs = {}, {}, {}

        def add(sums, key, new):
            sums[key] = sums[key] + new if key in sums else new

        def first(item):
            chain, c = item
            return dot(vs[chain[0]][c], operands[chain][1], NN)

        def second(item, dp):
            chain, c = item
            p, b, u = chain
            weight, _, qm, gm = operands[chain]
            block = target_blocks(n, rows).index(blocks[b])
            prob = exp_ref[first_pair + p, 2 * block + u, c].astype(F32) * weight
            ds = (prob * dp).astype(BF16)
            add(dvs, (p, c), dot(prob.astype(BF16), gm, NN))
            add(dks, (p, c), dot(ds, qm, NN))
            add(dqs, chain, dot(kt[p][c][u * HEAD_DIM : (u + 1) * HEAD_DIM], ds, NN))

        def store(p):
            lanes = slice(p * PAIR, (p + 1) * PAIR)
            half = count // 2
            for c in range(half):
                at = slice(c * size, (c + 1) * size)
                dk_own[0, at, lanes] = dks[p, c].astype(BF16)
                dv_own[0, at, lanes] = dvs[p, c].astype(BF16)
                d_oth[0, at, lanes] = dks[p, half + c].astype(BF16)
                d_oth[1, at, lanes] = dvs[p, half + c].astype(BF16)

        chains = [(p, b, u) for p in range(pairs) for b in range(len(blocks)) for u in range(2)]
        items = [(chain, c) for chain in chains for c in range(count)]
        ahead = first(items[0])
        for i, item in enumerate(items):
            now = ahead
            if i + 1 < len(items):
                ahead = first(items[i + 1])
            second(item, now)
            chain, c = item
            if c == count - 1:
                p, b, u = chain
                total = dqs[chain] * scale
                feat = slice(p * PAIR + u * HEAD_DIM, p * PAIR + (u + 1) * HEAD_DIM)
                for j, k in enumerate(blocks[b]):
                    dq[k][feat] = total[:, j * rows : (j + 1) * rows].astype(BF16)
                if i + 1 == len(items) or items[i + 1][0][0] != p:
                    store(p)
        for slots in rest:
            for k in slots:
                dq[k][...] = jnp.zeros_like(dq[k])

    for_valid_blocks(n, rows, info, run)


def context_kernel(n, rows, info, *refs):
    outs, stats, context = refs[:n], refs[n : 2 * n], refs[2 * n]
    lane = lax.broadcasted_iota(jnp.int32, (1, rows), 1)
    valid = (lane < slot_valid(info, n, rows, 0)).astype(F32)
    heads = outs[0].shape[0] // HEAD_DIM
    parts = []
    for head in range(heads):
        feat = slice(head * HEAD_DIM, (head + 1) * HEAD_DIM)
        lses = []
        for j in range(n):
            slot = 0 if rows % 128 else j
            lses.append(stats[j][head // 2, head % 2 : head % 2 + 1, slot * rows : (slot + 1) * rows])
        top = lses[0]
        for x in lses[1:]:
            top = jnp.maximum(top, x)
        weights = [jnp.exp(x - top) for x in lses]
        keep = valid / sum(weights)
        parts.append(sum(outs[j][feat].astype(F32) * (weights[j] * keep) for j in range(n)))
    context[...] = jnp.concatenate(parts, axis=0).T.astype(BF16)


def split_kernel(grad, pieces):
    width = pieces.shape[2]
    for k in range(pieces.shape[0]):
        pieces[k] = grad[:, k * width : (k + 1) * width]


def fill_kernel(info, back, dk_in, dv_in, dk, dv):
    dk[0] = back[0]
    dv[0] = back[1]


def finish_kernel(n, *refs):
    dq, pieces, out, context = refs[:n], refs[n], refs[n + 1], refs[n + 2]
    total = dq[0][...].astype(F32)
    for ref in dq[1:]:
        total = total + ref[...].astype(F32)
    out[...] = total.T.astype(BF16)
    width = pieces.shape[2]
    for k in range(pieces.shape[0]):
        context[:, k * width : (k + 1) * width] = pieces[k]


def compiler_params():
    return pltpu.CompilerParams(vmem_limit_bytes=VMEM_LIMIT)


def stay(x):
    return pltpu.with_memory_space_constraint(x, pltpu.HBM)


def xor_permute(x, axis, size, k):
    return lax.ppermute(x, axis, [(i, i ^ k) for i in range(size)])


def local(queries, keys, values, grad_out, pad_counts):
    rows, width = queries.shape
    src = keys.shape[1]
    n, m = lax.axis_size("seq"), lax.axis_size("head")
    group, seq = lax.axis_index("grp"), lax.axis_index("seq")
    sub = rows // m
    tgt = rows * n
    pairs = width // PAIR
    step = 2 if pairs % 2 == 0 else 1
    sds = jax.ShapeDtypeStruct
    whole = pl.BlockSpec(memory_space=pltpu.VMEM)
    smem = pl.BlockSpec(memory_space=pltpu.SMEM)
    anywhere = pl.BlockSpec(memory_space=pl.ANY)

    info = jnp.concatenate([group[None], seq[None], pad_counts]).astype(jnp.int32)

    def gather(x):
        return [x] + [xor_permute(x, "seq", n, k) for k in range(1, n)]

    def exchange(x):
        return lax.all_to_all(x, "head", split_axis=0, concat_axis=0, tiled=True)

    def plain(kernel, in_specs, out_shape, *args):
        out_specs = jax.tree.map(lambda x: whole, out_shape)
        return pl.pallas_call(
            kernel, in_specs=in_specs, out_specs=out_specs, out_shape=out_shape, compiler_params=compiler_params()
        )(*args)

    def call(kernel, in_specs, out_specs, out_shape, args, flops=0, alias={}):
        return pl.pallas_call(
            kernel,
            grid_spec=pltpu.PrefetchScalarGridSpec(
                num_scalar_prefetch=1, grid=(pairs // step,), in_specs=in_specs, out_specs=out_specs
            ),
            out_shape=out_shape,
            input_output_aliases=alias,
            compiler_params=compiler_params(),
            cost_estimate=pl.CostEstimate(flops=flops, bytes_accessed=1 << 20, transcendentals=0),
        )(info, *args)

    lanes = step * PAIR
    slot_in = [pl.BlockSpec((rows, lanes), lambda h, info: (0, h))] * n
    slot_t = [pl.BlockSpec((lanes, rows), lambda h, info: (h, 0))] * n
    own = pl.BlockSpec((1, src, lanes), lambda h, info: (info[0], 0, h))
    away = pl.BlockSpec((1, src, lanes), lambda h, info: (1 - info[0], 0, h))
    oth = pl.BlockSpec((2, src, lanes), lambda h, info: (0, 0, h))
    lse_spec = pl.BlockSpec((step, 2, tgt), lambda h, info: (h, 0, 0))
    out_spec = pl.BlockSpec((lanes, tgt), lambda h, info: (h, 0))
    stats_spec = pl.BlockSpec((step, 4, tgt), lambda h, info: (h, 0, 0))

    q = gather(queries)
    k_oth, v_oth = xor_permute(keys, "grp", 2, 1), xor_permute(values, "grp", 2, 1)
    pieces = plain(split_kernel, [whole], sds((m, sub, width), BF16), stay(grad_out))
    g = gather(exchange(pieces).reshape(rows, width))

    flop = 24 * tgt * 2 * src * width
    chunk, per = min(256, src), rows * len(target_blocks(n, rows)[0])
    exps = (pairs, 2 * (tgt // per), 2 * src // chunk, chunk, per)
    lse, top, out_t, exps = call(
        lambda *a: forward_kernel(n, rows, *a),
        slot_in + [own] * 4,
        [lse_spec, lse_spec, out_spec, whole],
        [sds((pairs, 2, tgt), F32)] * 2 + [sds((width, tgt), F32), sds(exps, BF16)],
        [stay(queries), *q[1:], stay(keys), stay(values), k_oth, v_oth],
        flops=2 * flop,
    )
    stats, *sends = plain(
        lambda *a: delta_kernel(n, rows, *a),
        [smem] + [whole] * (n + 2),
        [sds((pairs, 4, tgt), F32)] + [sds((width, rows), BF16)] * n,
        info, *g, lse, out_t,
    )
    all_stats = gather(stats)
    if rows % 128:

        def reorder(x, j):
            return x.reshape(pairs, 4, n, rows)[:, :, [k ^ j for k in range(n)]].reshape(pairs, 4, tgt)

        all_stats = [all_stats[0]] + [reorder(all_stats[j], j) for j in range(1, n)]
    outs = [sends[0]] + [xor_permute(sends[k], "seq", n, k) for k in range(1, n)]
    grads = call(
        lambda *a: backward_kernel(n, rows, *a),
        slot_in + slot_in + [stats_spec] * n + [own] * 4 + [lse_spec, whole],
        [own, own, oth] + slot_t,
        [sds((2, src, width), BF16)] * 3 + [sds((width, rows), BF16)] * n,
        [stay(queries), *q[1:], *g, *all_stats, stay(keys), stay(values), k_oth, v_oth, top, exps],
        flops=4 * flop,
    )
    (dk, dv, d_oth, *dq), outs = lax.optimization_barrier((grads, outs))
    dq = [dq[0]] + [xor_permute(dq[k], "seq", n, k) for k in range(1, n)]
    back = xor_permute(d_oth, "grp", 2, 1)

    context = plain(
        lambda *a: context_kernel(n, rows, *a),
        [smem] + [whole] * (2 * n),
        sds((rows, width), BF16),
        info, *outs, *all_stats,
    )
    pieces = exchange(context.reshape(m, sub, width))
    grad_keys, grad_values = call(
        fill_kernel,
        [oth, anywhere, anywhere],
        [away] * 2,
        [sds((2, src, width), BF16)] * 2,
        [back, dk, dv],
        alias={2: 0, 3: 1},
    )
    dq, grad_keys, grad_values = lax.optimization_barrier((dq, grad_keys, grad_values))
    grad_queries, context = plain(
        lambda *a: finish_kernel(n, *a),
        [whole] * (n + 1),
        [sds((rows, width), BF16), sds((sub, m * width), BF16)],
        *dq, pieces,
    )
    return (context, grad_queries, grad_keys, grad_values)


def solution(mesh):
    return jax.shard_map(
        local,
        mesh=mesh,
        in_specs=(
            P(("grp", "seq"), "head"),
            P(None, ("grp", "seq"), "head"),
            P(None, ("grp", "seq"), "head"),
            P(("grp", "seq", "head"), None),
            P(),
        ),
        out_specs=(
            P(("grp", "seq", "head"), None),
            P(("grp", "seq"), "head"),
            P(None, ("grp", "seq"), "head"),
            P(None, ("grp", "seq"), "head"),
        ),
        check_vma=False,
    )
```

time: 274 us -> 64.2 us (0.23)
  waiting for transfers between devices: 101 us -> 6.11 us
  blocking collectives: 52.6 us -> 0 us
  matrix products: 45 us -> 0 us
  local copies, waits for them, and re-layouts: 40.6 us -> 1.23 us
  starting transfers between devices: 11.2 us -> 35.3 us
  Pallas kernels: 0 us -> 19.7 us
  between operations: 14 us -> 0.72 us
  other arithmetic: 8.19 us -> 0.73 us
    psum x1 -> x0, waiting for transfers between devices: 58.4 us -> none  [local(): summed = lax.psum(partial_value, ('grp', 'seq'))]
    dot_general x28 -> x0, matrix products: 45 us -> none  [the longest x4 15.5 us: forward_step(): jnp.einsum('bhtp,bphd->bthd', probs.astype(jnp.bfloat16), value_block, pr...]
    reduce_scatter x1 -> x0, waiting for transfers between devices: 27 us -> none  [local(): lax.psum_scatter(grad_q.reshape(batch * seq_len, width), ('grp', 'seq'),...]
    pmax x1 -> x0, blocking collectives: 26.6 us -> none  [local(): row_top = lax.pmax(top, ('grp', 'seq'))]
    psum x1 -> x0, blocking collectives: 26 us -> none  [local(): row_total = lax.psum(total * jnp.exp(top - row_top), ('grp', 'seq'))]
    ppermute x0 -> x18, starting transfers between devices: none -> 24.3 us  [xor_permute(): return lax.ppermute(x, axis, [(i, i ^ k) for i in range(size)])]
    pallas_call x0 -> x7, Pallas kernels: none -> 19.7 us  [the longest x3 15 us: call(): pl.pallas_call(kernel, grid_spec=pltpu.PrefetchScalarGridSpec(num_scalar_...]
    unnamed x21 -> x4, local copies, waits for them, and re-layouts: 18.2 us -> 1.23 us
  transfers between devices with their start and end apart: 6 -> 20, of which waited for: 4 -> 3; matrix products, arithmetic and copies ran while one was open for 19% -> 1% of each run, Pallas kernels for 0% -> 28%
where the time goes in v1:
time: 64.2 us; the launch traced here: 63.7 us
  starting transfers between devices  35.3 us (55%)
  Pallas kernels  19.7 us (31%)
  waiting for transfers between devices  6.11 us (10%)
  local copies, waits for them, and re-layouts  1.23 us (2%)
  other arithmetic  0.73 us (1%)
  between operations  0.72 us (1%)
    ppermute x18, starting transfers between devices, xor_permute(): return lax.ppermute(x, axis, [(i, i ^ k) for i in range(size)])  24.3 us
    pallas_call x3, Pallas kernels, call(): pl.pallas_call(kernel, grid_spec=pltpu.PrefetchScalarGridSpec(num_scalar_...  15 us
    all_to_all x2, starting transfers between devices, exchange(): return lax.all_to_all(x, 'head', split_axis=0, concat_axis=0, tiled=True)  11 us
    ppermute x18, waiting for transfers between devices, xor_permute(): return lax.ppermute(x, axis, [(i, i ^ k) for i in range(size)])  6.11 us
    pallas_call x4, Pallas kernels, plain(): pl.pallas_call(kernel, in_specs=in_specs, out_specs=out_specs, out_shape=...  4.7 us
  transfers between devices with their start and end apart: 20, of which 3 were waited for; matrix products, arithmetic and copies ran while one was open for 1% of the time, Pallas kernels for 28%

profile of v1, /device:TPU:0, one launch (start us, length us, event | category | flops | bytes accessed | tf_op | source)
XLA Modules:
  0.0 63.7 jit_solution(10277696523166968127)
XLA Ops:
  0.6 0.5 collective-permute-start.6
  1.1 0.1 collective-permute-start.7
  1.2 1.6 %shard_map.84 = bf16[4,32,512]{2,1,0:T(8,128)(2,1)} custom-call(bf16[32,2048]{1,0:T(8,128)(2,1)} %grad.1), custom_call_target="tpu_custom_call" | custom-call | tf_op jit(solution)/shard_map/pallas_call | solution.py:360
  2.8 6.3 %all-to-all-start = ((bf16[4,32,512]{2,1,0:T(8,128)(2,1)}), bf16[4,32,512]{2,1,0:T(8,128)(2,1)S(1)}, u32[]{:S(2)}, u32[]{:S(2)}) async-start(bf16[4,32,512]{2,1,0:T(8,128)(2,1)} %shard_map.84), calls=%async_computation | async-start | bytes 262144 | tf_op jit(solution)/shard_map/all_to_all | solution.py:356
  9.1 2.4 %collective-permute-start.2 = (bf16[128,512]{1,0:T(8,128)(2,1)}, bf16[128,512]{1,0:T(8,128)(2,1)S(1)}, u32[]{:S(2)}, u32[]{:S(2)}) collective-permute-start(bf16[128,512]{1,0:T(8,128)(2,1)} %a_1_.3), channel_id=1, source_target_pairs={{0,12},{4,8},{8,4},{12,0},{1,13},{5,9},{9,5},{13,1},{2,14},{6,10},... | collective-permute-start | bytes 393224 | tf_op jit(solution)/shard_map/ppermute | solution.py:333
  11.5 0.5 collective-permute-start.1
  12.0 0.5 collective-permute-start
  12.6 0.7 %pad_add_fusion.a_0_.info = s32[4]{0:T(128)S(1)} fusion(s32[2]{0:T(128)} %param.9, s32[1]{0:T(128)} %bitcast.1, s32[1]{0:T(128)} %bitcast), kind=kLoop, calls=%fused_computation | loop fusion | flops 8 | bytes 32 | tf_op jit(solution)/shard_map/concatenate | solution.py:350
  13.3 2.5 %collective-permute-done.2.a_4_ = bf16[128,512]{1,0:T(8,128)(2,1)S(1)} collective-permute-done((bf16[128,512]{1,0:T(8,128)(2,1)}, bf16[128,512]{1,0:T(8,128)(2,1)S(1)}, u32[]{:S(2)}, u32[]{:S(2)}) %collective-permute-start.2) | collective-permute-done | bytes 131104 | tf_op jit(solution)/shard_map/ppermute | solution.py:333
  15.8 0.0 all-to-all-done
  15.8 3.3 %collective-permute-start.5 = (bf16[128,512]{1,0:T(8,128)(2,1)S(1)}, bf16[128,512]{1,0:T(8,128)(2,1)S(1)}, u32[]{:S(2)}, u32[]{:S(2)}) collective-permute-start(bf16[128,512]{1,0:T(8,128)(2,1)S(1)} %bitcast.4), channel_id=1, source_target_pairs={{0,12},{4,8},{8,4},{12,0},{1,13},{5,9},{9,5},{13,1},{2,14},{6,10},... | collective-permute-start | bytes 393224 | tf_op jit(solution)/shard_map/ppermute | solution.py:333
  19.0 0.0 collective-permute-done.1.a_3_
  19.1 1.0 %collective-permute-start.4 = (bf16[128,512]{1,0:T(8,128)(2,1)S(1)}, bf16[128,512]{1,0:T(8,128)(2,1)S(1)}, u32[]{:S(2)}, u32[]{:S(2)}) collective-permute-start(bf16[128,512]{1,0:T(8,128)(2,1)S(1)} %bitcast.5), channel_id=1, source_target_pairs={{0,8},{4,12},{8,0},{12,4},{1,9},{5,13},{9,1},{13,5},{2,10},{6,14},... | collective-permute-start | bytes 393224 | tf_op jit(solution)/shard_map/ppermute | solution.py:333
  20.1 0.0 collective-permute-done.a_2_
  20.1 0.5 collective-permute-start.3
  20.5 0.0 collective-permute-done.6.a_7_.a_15_
  20.5 0.0 collective-permute-done.7.a_8_.a_16_
  20.5 5.4 %shard_map.85 = (f32[4,2,512]{2,1,0:T(2,128)S(1)}, f32[4,2,512]{2,1,0:T(2,128)S(1)}, f32[512,512]{1,0:T(8,128)S(1)}, bf16[4,4,4,256,256]{4,3,2,1,0:T(8,128)(2,1)S(1)}) custom-call(s32[4]{0:T(128)S(1)} %pad_add_fusion.a_0_.info, bf16[128,512]{1,0:T(8,128)(2,1)} %a_1_.3, bf16[128,512]{1,0:T(8,128)(2,1)S(1)} %collective-permute-done.a_2_, ...), custom_call_target="tpu_custom_call" | custom-call | flops 12884901888 | bytes 1048576 | tf_op jit(solution)/shard_map/pallas_call | solution.py:365
  25.9 0.0 collective-permute-done.5.a_4_.a_8_
  26.0 0.0 collective-permute-done.4.a_3_.a_7_
  26.0 0.0 collective-permute-done.3.a_2_.a_6_
  26.0 0.9 %shard_map.86 = (f32[4,4,512]{2,1,0:T(4,128)S(1)}, bf16[512,128]{1,0:T(8,128)(2,1)S(1)}, bf16[512,128]{1,0:T(8,128)(2,1)S(1)}, bf16[512,128]{1,0:T(8,128)(2,1)S(1)}, bf16[512,128]{1,0:T(8,128)(2,1)S(1)}) custom-call(s32[4]{0:T(128)S(1)} %pad_add_fusion.a_0_.info, bf16[128,512]{1,0:T(8,128)(2,1)S(1)} %bitcast.7, ...), custom_call_target="tpu_custom_call" | custom-call | tf_op jit(solution)/shard_map/pallas_call | solution.py:360
  26.9 2.1 %collective-permute-start.10 = (f32[4,4,512]{2,1,0:T(4,128)S(1)}, f32[4,4,512]{2,1,0:T(4,128)S(1)}, u32[]{:S(2)}, u32[]{:S(2)}) collective-permute-start(f32[4,4,512]{2,1,0:T(4,128)S(1)} %get-tuple-element.43.a_9_.a_5_), channel_id=1, source_target_pairs={{0,12},{4,8},{8,4},{12,0},{1,13},{5,9},{9,5},{13,1},{2,14},{6,10},... | collective-permute-start | bytes 98312 | tf_op jit(solution)/shard_map/ppermute | solution.py:333
  29.0 1.0 %collective-permute-start.9 = (f32[4,4,512]{2,1,0:T(4,128)S(1)}, f32[4,4,512]{2,1,0:T(4,128)S(1)}, u32[]{:S(2)}, u32[]{:S(2)}) collective-permute-start(f32[4,4,512]{2,1,0:T(4,128)S(1)} %get-tuple-element.43.a_9_.a_5_), channel_id=1, source_target_pairs={{0,8},{4,12},{8,0},{12,4},{1,9},{5,13},{9,1},{13,5},{2,10},{6,14},... | collective-permute-start | bytes 98312 | tf_op jit(solution)/shard_map/ppermute | solution.py:333
  30.0 0.5 collective-permute-start.8
  30.5 1.6 %collective-permute-start.11 = (bf16[512,128]{1,0:T(8,128)(2,1)S(1)}, bf16[512,128]{1,0:T(8,128)(2,1)S(1)}, u32[]{:S(2)}, u32[]{:S(2)}) collective-permute-start(bf16[512,128]{1,0:T(8,128)(2,1)S(1)} %get-tuple-element.54), channel_id=1, source_target_pairs={{0,4},{4,0},{8,12},{12,8},{1,5},{5,1},{9,13},{13,9},{2,6},{6,2},{1... | collective-permute-start | bytes 393224 | tf_op jit(solution)/shard_map/ppermute | solution.py:333
  32.0 1.0 %collective-permute-start.12 = (bf16[512,128]{1,0:T(8,128)(2,1)S(1)}, bf16[512,128]{1,0:T(8,128)(2,1)S(1)}, u32[]{:S(2)}, u32[]{:S(2)}) collective-permute-start(bf16[512,128]{1,0:T(8,128)(2,1)S(1)} %get-tuple-element.55), channel_id=1, source_target_pairs={{0,8},{4,12},{8,0},{12,4},{1,9},{5,13},{9,1},{13,5},{2,10},{6,14},... | collective-permute-start | bytes 393224 | tf_op jit(solution)/shard_map/ppermute | solution.py:333
  33.0 0.0 collective-permute-done.10.a_12_.a_8_
  33.0 0.9 %collective-permute-start.13 = (bf16[512,128]{1,0:T(8,128)(2,1)S(1)}, bf16[512,128]{1,0:T(8,128)(2,1)S(1)}, u32[]{:S(2)}, u32[]{:S(2)}) collective-permute-start(bf16[512,128]{1,0:T(8,128)(2,1)S(1)} %get-tuple-element.56), channel_id=1, source_target_pairs={{0,12},{4,8},{8,4},{12,0},{1,13},{5,9},{9,5},{13,1},{2,14},{6,10},... | collective-permute-start | bytes 393224 | tf_op jit(solution)/shard_map/ppermute | solution.py:333
  33.9 0.0 collective-permute-done.9.a_11_.a_7_
  33.9 0.0 collective-permute-done.8.a_10_.a_6_
  34.0 1.2 %copy-done.1 = bf16[2,512,512]{2,1,0:T(8,128)(2,1)S(1)} copy-done((bf16[2,512,512]{2,1,0:T(8,128)(2,1)S(1)}, bf16[2,512,512]{2,1,0:T(8,128)(2,1)}, u32[]{:S(2)}) %copy-start.1) | copy-done | bytes 1048600
  35.2 7.9 %shard_map.87 = (bf16[2,512,512]{2,1,0:T(8,128)(2,1)}, bf16[2,512,512]{2,1,0:T(8,128)(2,1)}, bf16[2,512,512]{2,1,0:T(8,128)(2,1)}, bf16[512,128]{1,0:T(8,128)(2,...) custom-call(s32[4]{0:T(128)S(1)} %pad_add_fusion.a_0_.info, ...), custom_call_target="tpu_custom_call" | custom-call | flops 25769803776 | bytes 1048576 | tf_op jit(solution)/shard_map/pallas_call | solution.py:365
  43.1 0.0 collective-permute-done.11.a_2_
  43.1 0.0 collective-permute-done.12.a_3_
  43.1 0.0 collective-permute-done.13.a_4_
  43.1 4.9 %collective-permute-start.17 = (bf16[2,512,512]{2,1,0:T(8,128)(2,1)}, bf16[2,512,512]{2,1,0:T(8,128)(2,1)S(1)}, u32[]{:S(2)}, u32[]{:S(2)}) collective-permute-start(bf16[2,512,512]{2,1,0:T(8,128)(2,1)} %get-tuple-element.61), channel_id=1, source_target_pairs={{0,16},{16,0},{1,17},{17,1},{2,18},{18,2},{3,19},{19,3},{4,20},{20... | collective-permute-start | bytes 3145736 | tf_op jit(solution)/shard_map/ppermute | solution.py:333
  48.1 1.4 %shard_map.89 = bf16[128,512]{1,0:T(8,128)(2,1)} custom-call(s32[4]{0:T(128)S(1)} %pad_add_fusion.a_0_.info, bf16[512,128]{1,0:T(8,128)(2,1)S(1)} %get-tuple-element.70.a_1_, bf16[512,128]{1,0:T(8,128)(2,1)S(1)} %collective-permute-done.11.a_2_, bf16[512,128]{1,0:T(8,128)(2,1)S(1)} %collective-permute-done.12.a_3_, ...), custom_call_target="tpu_custom_call" | custom-call | tf_op jit(solution)/shard_map/pallas_call | solution.py:360
  49.5 4.7 %all-to-all-start.1 = ((bf16[4,32,512]{2,1,0:T(8,128)(2,1)}), bf16[4,32,512]{2,1,0:T(8,128)(2,1)S(1)}, u32[]{:S(2)}, u32[]{:S(2)}) async-start(bf16[4,32,512]{2,1,0:T(8,128)(2,1)} %bitcast.3), calls=%async_computation.1 | async-start | bytes 262144 | tf_op jit(solution)/shard_map/all_to_all | solution.py:356
  54.2 1.1 %collective-permute-start.14 = (bf16[512,128]{1,0:T(8,128)(2,1)S(1)}, bf16[512,128]{1,0:T(8,128)(2,1)S(1)}, u32[]{:S(2)}, u32[]{:S(2)}) collective-permute-start(bf16[512,128]{1,0:T(8,128)(2,1)S(1)} %get-tuple-element.58), channel_id=1, source_target_pairs={{0,4},{4,0},{8,12},{12,8},{1,5},{5,1},{9,13},{13,9},{2,6},{6,2},{1... | collective-permute-start | bytes 393224 | tf_op jit(solution)/shard_map/ppermute | solution.py:333
  55.3 0.7 %collective-permute-start.15 = (bf16[512,128]{1,0:T(8,128)(2,1)S(1)}, bf16[512,128]{1,0:T(8,128)(2,1)S(1)}, u32[]{:S(2)}, u32[]{:S(2)}) collective-permute-start(bf16[512,128]{1,0:T(8,128)(2,1)S(1)} %get-tuple-element.59), channel_id=1, source_target_pairs={{0,8},{4,12},{8,0},{12,4},{1,9},{5,13},{9,1},{13,5},{2,10},{6,14},... | collective-permute-start | bytes 393224 | tf_op jit(solution)/shard_map/ppermute | solution.py:333
  55.9 1.7 %collective-permute-start.16 = (bf16[512,128]{1,0:T(8,128)(2,1)S(1)}, bf16[512,128]{1,0:T(8,128)(2,1)S(1)}, u32[]{:S(2)}, u32[]{:S(2)}) collective-permute-start(bf16[512,128]{1,0:T(8,128)(2,1)S(1)} %get-tuple-element.60), channel_id=1, source_target_pairs={{0,12},{4,8},{8,4},{12,0},{1,13},{5,9},{9,5},{13,1},{2,14},{6,10},... | collective-permute-start | bytes 393224 | tf_op jit(solution)/shard_map/ppermute | solution.py:333
  57.7 0.0 collective-permute-done.17.back
  57.7 1.7 %shard_map.88 = (bf16[2,512,512]{2,1,0:T(8,128)(2,1)}, bf16[2,512,512]{2,1,0:T(8,128)(2,1)}) custom-call(s32[4]{0:T(128)S(1)} %pad_add_fusion.a_0_.info, bf16[2,512,512]{2,1,0:T(8,128)(2,1)S(1)} %collective-permute-done.17.back, bf16[2,512,512]{2,1,0:T(8,128)(2,1)} %get-tuple-element.62.dk_in, ...), custom_call_target="tpu_custom_call", output_to_operand_aliasing={{0}: (2, {}), {1}: (3, {})} | custom-call | bytes 1048576 | tf_op jit(solution)/shard_map/pallas_call | solution.py:365
  59.3 0.8 %collective-permute-done.14.a_1_ = bf16[512,128]{1,0:T(8,128)(2,1)S(1)} collective-permute-done((bf16[512,128]{1,0:T(8,128)(2,1)S(1)}, bf16[512,128]{1,0:T(8,128)(2,1)S(1)}, u32[]{:S(2)}, u32[]{:S(2)}) %collective-permute-start.14) | collective-permute-done | bytes 131104 | tf_op jit(solution)/shard_map/ppermute | solution.py:333
  60.1 2.8 %collective-permute-done.15.a_2_ = bf16[512,128]{1,0:T(8,128)(2,1)S(1)} collective-permute-done((bf16[512,128]{1,0:T(8,128)(2,1)S(1)}, bf16[512,128]{1,0:T(8,128)(2,1)S(1)}, u32[]{:S(2)}, u32[]{:S(2)}) %collective-permute-start.15) | collective-permute-done | bytes 131104 | tf_op jit(solution)/shard_map/ppermute | solution.py:333
  62.9 0.0 collective-permute-done.16.a_3_
  62.9 0.8 %shard_map.90 = (bf16[128,512]{1,0:T(8,128)(2,1)}, bf16[32,2048]{1,0:T(8,128)(2,1)}) custom-call(bf16[512,128]{1,0:T(8,128)(2,1)S(1)} %get-tuple-element.66.a_0_, bf16[512,128]{1,0:T(8,128)(2,1)S(1)} %collective-permute-done.14.a_1_, bf16[512,128]{1,0:T(8,128)(2,1)S(1)} %collective-permute-done.15.a_2_, bf16[512,128]{1,0:T(8,128)(2,1)S(1)} %collective-permute-done.16.a_3_, ...), custom_call_target="tpu_custom_call" | custom-call | tf_op jit(solution)/shard_map/pallas_call | solution.py:360
  (4 shorter events, 0.0 us)
Async XLA Ops:
  0.6 19.9 %collective-permute-start.6 = (bf16[2,512,512]{2,1,0:T(8,128)(2,1)}, bf16[2,512,512]{2,1,0:T(8,128)(2,1)S(1)}, u32[]{:S(2)}, u32[]{:S(2)}) collective-permute-start(bf16[2,512,512]{2,1,0:T(8,128)(2,1)} %a_13_.1), channel_id=1, source_target_pairs={{0,16},{16,0},{1,17},{17,1},{2,18},{18,2},{3,19},{19,3},{4,20},{20... | collective-permute-start | bytes 3145736 | tf_op jit(solution)/shard_map/ppermute | solution.py:333
  1.1 19.4 %collective-permute-start.7 = (bf16[2,512,512]{2,1,0:T(8,128)(2,1)}, bf16[2,512,512]{2,1,0:T(8,128)(2,1)S(1)}, u32[]{:S(2)}, u32[]{:S(2)}) collective-permute-start(bf16[2,512,512]{2,1,0:T(8,128)(2,1)} %a_14_.1), channel_id=1, source_target_pairs={{0,16},{16,0},{1,17},{17,1},{2,18},{18,2},{3,19},{19,3},{4,20},{20... | collective-permute-start | bytes 3145736 | tf_op jit(solution)/shard_map/ppermute | solution.py:333
  2.8 13.0 %all-to-all-start = ((bf16[4,32,512]{2,1,0:T(8,128)(2,1)}), bf16[4,32,512]{2,1,0:T(8,128)(2,1)S(1)}, u32[]{:S(2)}, u32[]{:S(2)}) async-start(bf16[4,32,512]{2,1,0:T(8,128)(2,1)} %shard_map.84), calls=%async_computation | async-start | bytes 262144 | tf_op jit(solution)/shard_map/all_to_all | solution.py:356
  9.1 6.7 %collective-permute-start.2 = (bf16[128,512]{1,0:T(8,128)(2,1)}, bf16[128,512]{1,0:T(8,128)(2,1)S(1)}, u32[]{:S(2)}, u32[]{:S(2)}) collective-permute-start(bf16[128,512]{1,0:T(8,128)(2,1)} %a_1_.3), channel_id=1, source_target_pairs={{0,12},{4,8},{8,4},{12,0},{1,13},{5,9},{9,5},{13,1},{2,14},{6,10},... | collective-permute-start | bytes 393224 | tf_op jit(solution)/shard_map/ppermute | solution.py:333
  11.5 7.5 %collective-permute-start.1 = (bf16[128,512]{1,0:T(8,128)(2,1)}, bf16[128,512]{1,0:T(8,128)(2,1)S(1)}, u32[]{:S(2)}, u32[]{:S(2)}) collective-permute-start(bf16[128,512]{1,0:T(8,128)(2,1)} %a_1_.3), channel_id=1, source_target_pairs={{0,8},{4,12},{8,0},{12,4},{1,9},{5,13},{9,1},{13,5},{2,10},{6,14},... | collective-permute-start | bytes 393224 | tf_op jit(solution)/shard_map/ppermute | solution.py:333
  12.0 8.0 %collective-permute-start = (bf16[128,512]{1,0:T(8,128)(2,1)}, bf16[128,512]{1,0:T(8,128)(2,1)S(1)}, u32[]{:S(2)}, u32[]{:S(2)}) collective-permute-start(bf16[128,512]{1,0:T(8,128)(2,1)} %a_1_.3), channel_id=1, source_target_pairs={{0,4},{4,0},{8,12},{12,8},{1,5},{5,1},{9,13},{13,9},{2,6},{6,2},{1... | collective-permute-start | bytes 393224 | tf_op jit(solution)/shard_map/ppermute | solution.py:333
  15.8 10.2 %collective-permute-start.5 = (bf16[128,512]{1,0:T(8,128)(2,1)S(1)}, bf16[128,512]{1,0:T(8,128)(2,1)S(1)}, u32[]{:S(2)}, u32[]{:S(2)}) collective-permute-start(bf16[128,512]{1,0:T(8,128)(2,1)S(1)} %bitcast.4), channel_id=1, source_target_pairs={{0,12},{4,8},{8,4},{12,0},{1,13},{5,9},{9,5},{13,1},{2,14},{6,10},... | collective-permute-start | bytes 393224 | tf_op jit(solution)/shard_map/ppermute | solution.py:333
  19.1 6.9 %collective-permute-start.4 = (bf16[128,512]{1,0:T(8,128)(2,1)S(1)}, bf16[128,512]{1,0:T(8,128)(2,1)S(1)}, u32[]{:S(2)}, u32[]{:S(2)}) collective-permute-start(bf16[128,512]{1,0:T(8,128)(2,1)S(1)} %bitcast.5), channel_id=1, source_target_pairs={{0,8},{4,12},{8,0},{12,4},{1,9},{5,13},{9,1},{13,5},{2,10},{6,14},... | collective-permute-start | bytes 393224 | tf_op jit(solution)/shard_map/ppermute | solution.py:333
  20.1 5.9 %collective-permute-start.3 = (bf16[128,512]{1,0:T(8,128)(2,1)S(1)}, bf16[128,512]{1,0:T(8,128)(2,1)S(1)}, u32[]{:S(2)}, u32[]{:S(2)}) collective-permute-start(bf16[128,512]{1,0:T(8,128)(2,1)S(1)} %bitcast.6), channel_id=1, source_target_pairs={{0,4},{4,0},{8,12},{12,8},{1,5},{5,1},{9,13},{13,9},{2,6},{6,2},{1... | collective-permute-start | bytes 393224 | tf_op jit(solution)/shard_map/ppermute | solution.py:333
  20.5 5.4 %copy-start = (bf16[2,512,512]{2,1,0:T(8,128)(2,1)}, bf16[2,512,512]{2,1,0:T(8,128)(2,1)S(1)}, u32[]{:S(2)}) copy-start(bf16[2,512,512]{2,1,0:T(8,128)(2,1)S(1)} %collective-permute-done.7.a_8_.a_16_) | copy-start | bytes 3145732
  26.9 6.1 %collective-permute-start.10 = (f32[4,4,512]{2,1,0:T(4,128)S(1)}, f32[4,4,512]{2,1,0:T(4,128)S(1)}, u32[]{:S(2)}, u32[]{:S(2)}) collective-permute-start(f32[4,4,512]{2,1,0:T(4,128)S(1)} %get-tuple-element.43.a_9_.a_5_), channel_id=1, source_target_pairs={{0,12},{4,8},{8,4},{12,0},{1,13},{5,9},{9,5},{13,1},{2,14},{6,10},... | collective-permute-start | bytes 98312 | tf_op jit(solution)/shard_map/ppermute | solution.py:333
  29.0 5.0 %collective-permute-start.9 = (f32[4,4,512]{2,1,0:T(4,128)S(1)}, f32[4,4,512]{2,1,0:T(4,128)S(1)}, u32[]{:S(2)}, u32[]{:S(2)}) collective-permute-start(f32[4,4,512]{2,1,0:T(4,128)S(1)} %get-tuple-element.43.a_9_.a_5_), channel_id=1, source_target_pairs={{0,8},{4,12},{8,0},{12,4},{1,9},{5,13},{9,1},{13,5},{2,10},{6,14},... | collective-permute-start | bytes 98312 | tf_op jit(solution)/shard_map/ppermute | solution.py:333
  30.0 4.0 %collective-permute-start.8 = (f32[4,4,512]{2,1,0:T(4,128)S(1)}, f32[4,4,512]{2,1,0:T(4,128)S(1)}, u32[]{:S(2)}, u32[]{:S(2)}) collective-permute-start(f32[4,4,512]{2,1,0:T(4,128)S(1)} %get-tuple-element.43.a_9_.a_5_), channel_id=1, source_target_pairs={{0,4},{4,0},{8,12},{12,8},{1,5},{5,1},{9,13},{13,9},{2,6},{6,2},{1... | collective-permute-start | bytes 98312 | tf_op jit(solution)/shard_map/ppermute | solution.py:333
  30.5 12.7 %collective-permute-start.11 = (bf16[512,128]{1,0:T(8,128)(2,1)S(1)}, bf16[512,128]{1,0:T(8,128)(2,1)S(1)}, u32[]{:S(2)}, u32[]{:S(2)}) collective-permute-start(bf16[512,128]{1,0:T(8,128)(2,1)S(1)} %get-tuple-element.54), channel_id=1, source_target_pairs={{0,4},{4,0},{8,12},{12,8},{1,5},{5,1},{9,13},{13,9},{2,6},{6,2},{1... | collective-permute-start | bytes 393224 | tf_op jit(solution)/shard_map/ppermute | solution.py:333
  32.0 11.1 %collective-permute-start.12 = (bf16[512,128]{1,0:T(8,128)(2,1)S(1)}, bf16[512,128]{1,0:T(8,128)(2,1)S(1)}, u32[]{:S(2)}, u32[]{:S(2)}) collective-permute-start(bf16[512,128]{1,0:T(8,128)(2,1)S(1)} %get-tuple-element.55), channel_id=1, source_target_pairs={{0,8},{4,12},{8,0},{12,4},{1,9},{5,13},{9,1},{13,5},{2,10},{6,14},... | collective-permute-start | bytes 393224 | tf_op jit(solution)/shard_map/ppermute | solution.py:333
  33.0 10.1 %collective-permute-start.13 = (bf16[512,128]{1,0:T(8,128)(2,1)S(1)}, bf16[512,128]{1,0:T(8,128)(2,1)S(1)}, u32[]{:S(2)}, u32[]{:S(2)}) collective-permute-start(bf16[512,128]{1,0:T(8,128)(2,1)S(1)} %get-tuple-element.56), channel_id=1, source_target_pairs={{0,12},{4,8},{8,4},{12,0},{1,13},{5,9},{9,5},{13,1},{2,14},{6,10},... | collective-permute-start | bytes 393224 | tf_op jit(solution)/shard_map/ppermute | solution.py:333
  34.0 1.2 %copy-start.1 = (bf16[2,512,512]{2,1,0:T(8,128)(2,1)S(1)}, bf16[2,512,512]{2,1,0:T(8,128)(2,1)}, u32[]{:S(2)}) copy-start(bf16[2,512,512]{2,1,0:T(8,128)(2,1)} %copy-done) | copy-start | bytes 3145732
  43.1 14.5 %collective-permute-start.17 = (bf16[2,512,512]{2,1,0:T(8,128)(2,1)}, bf16[2,512,512]{2,1,0:T(8,128)(2,1)S(1)}, u32[]{:S(2)}, u32[]{:S(2)}) collective-permute-start(bf16[2,512,512]{2,1,0:T(8,128)(2,1)} %get-tuple-element.61), channel_id=1, source_target_pairs={{0,16},{16,0},{1,17},{17,1},{2,18},{18,2},{3,19},{19,3},{4,20},{20... | collective-permute-start | bytes 3145736 | tf_op jit(solution)/shard_map/ppermute | solution.py:333
  49.5 13.4 %all-to-all-start.1 = ((bf16[4,32,512]{2,1,0:T(8,128)(2,1)}), bf16[4,32,512]{2,1,0:T(8,128)(2,1)S(1)}, u32[]{:S(2)}, u32[]{:S(2)}) async-start(bf16[4,32,512]{2,1,0:T(8,128)(2,1)} %bitcast.3), calls=%async_computation.1 | async-start | bytes 262144 | tf_op jit(solution)/shard_map/all_to_all | solution.py:356
  54.2 6.0 %collective-permute-start.14 = (bf16[512,128]{1,0:T(8,128)(2,1)S(1)}, bf16[512,128]{1,0:T(8,128)(2,1)S(1)}, u32[]{:S(2)}, u32[]{:S(2)}) collective-permute-start(bf16[512,128]{1,0:T(8,128)(2,1)S(1)} %get-tuple-element.58), channel_id=1, source_target_pairs={{0,4},{4,0},{8,12},{12,8},{1,5},{5,1},{9,13},{13,9},{2,6},{6,2},{1... | collective-permute-start | bytes 393224 | tf_op jit(solution)/shard_map/ppermute | solution.py:333
  55.3 7.7 %collective-permute-start.15 = (bf16[512,128]{1,0:T(8,128)(2,1)S(1)}, bf16[512,128]{1,0:T(8,128)(2,1)S(1)}, u32[]{:S(2)}, u32[]{:S(2)}) collective-permute-start(bf16[512,128]{1,0:T(8,128)(2,1)S(1)} %get-tuple-element.59), channel_id=1, source_target_pairs={{0,8},{4,12},{8,0},{12,4},{1,9},{5,13},{9,1},{13,5},{2,10},{6,14},... | collective-permute-start | bytes 393224 | tf_op jit(solution)/shard_map/ppermute | solution.py:333
  55.9 7.0 %collective-permute-start.16 = (bf16[512,128]{1,0:T(8,128)(2,1)S(1)}, bf16[512,128]{1,0:T(8,128)(2,1)S(1)}, u32[]{:S(2)}, u32[]{:S(2)}) collective-permute-start(bf16[512,128]{1,0:T(8,128)(2,1)S(1)} %get-tuple-element.60), channel_id=1, source_target_pairs={{0,12},{4,8},{8,4},{12,0},{1,13},{5,9},{9,5},{13,1},{2,14},{6,10},... | collective-permute-start | bytes 393224 | tf_op jit(solution)/shard_map/ppermute | solution.py:333

commit v2 on v1

--- a/solution.py
+++ b/solution.py
@@ -12,7 +12,7 @@
 LOG2E = math.log2(math.e)
 F32 = jnp.float32
 BF16 = jnp.bfloat16
-VMEM_LIMIT = 28 * 1024 * 1024
+VMEM_LIMIT = 16 * 1024 * 1024
 
 NT = (((1,), (1,)), ((), ()))
 NN = (((1,), (0,)), ((), ()))
@@ -299,10 +299,16 @@
     context[...] = jnp.concatenate(parts, axis=0).T.astype(BF16)
 
 
-def split_kernel(grad, pieces):
+def split_kernel(grad, pieces, sems):
     width = pieces.shape[2]
-    for k in range(pieces.shape[0]):
-        pieces[k] = grad[:, k * width : (k + 1) * width]
+    copies = [
+        pltpu.make_async_copy(grad.at[:, k * width : (k + 1) * width], pieces.at[k], sems.at[k])
+        for k in range(pieces.shape[0])
+    ]
+    for c in copies:
+        c.start()
+    for c in copies:
+        c.wait()
 
 
 def fill_kernel(info, back, dk_in, dv_in, dk, dv):
@@ -385,7 +391,13 @@
 
     q = gather(queries)
     k_oth, v_oth = xor_permute(keys, "grp", 2, 1), xor_permute(values, "grp", 2, 1)
-    pieces = plain(split_kernel, [whole], sds((m, sub, width), BF16), stay(grad_out))
+    pieces = pl.pallas_call(
+        split_kernel,
+        in_specs=[pl.BlockSpec(memory_space=pltpu.HBM)],
+        out_specs=whole,
+        out_shape=sds((m, sub, width), BF16),
+        scratch_shapes=[pltpu.SemaphoreType.DMA((m,))],
+    )(stay(grad_out))
     g = gather(exchange(pieces).reshape(rows, width))
 
     flop = 24 * tgt * 2 * src * width

time: 64.2 us -> 62.5 us (0.974); the launches traced: 63.7 us -> 63.8 us
    pallas_call x4 -> x3, Pallas kernels: 4.7 us -> 3.13 us  [plain(): pl.pallas_call(kernel, in_specs=in_specs, out_specs=out_specs, out_shape=...]
    pallas_call x0 -> x1, Pallas kernels: none -> 1.49 us  [local(): pl.pallas_call(split_kernel, in_specs=[pl.BlockSpec(memory_space=pltpu.HB...]
where the time goes in v2:
time: 62.5 us; the launch traced here: 63.8 us
  starting transfers between devices  35.4 us (57%)
  Pallas kernels  19.6 us (31%)
  waiting for transfers between devices  6.1 us (10%)
  local copies, waits for them, and re-layouts  1.23 us (2%)
  other arithmetic  0.73 us (1%)
  between operations  0.73 us (1%)
    ppermute x18, starting transfers between devices, xor_permute(): return lax.ppermute(x, axis, [(i, i ^ k) for i in range(size)])  24.3 us
    pallas_call x3, Pallas kernels, call(): pl.pallas_call(kernel, grid_spec=pltpu.PrefetchScalarGridSpec(num_scalar_...  15 us
    all_to_all x2, starting transfers between devices, exchange(): return lax.all_to_all(x, 'head', split_axis=0, concat_axis=0, tiled=True)  11 us
    ppermute x18, waiting for transfers between devices, xor_permute(): return lax.ppermute(x, axis, [(i, i ^ k) for i in range(size)])  6.1 us
    pallas_call x3, Pallas kernels, plain(): pl.pallas_call(kernel, in_specs=in_specs, out_specs=out_specs, out_shape=...  3.13 us
    pallas_call x1, Pallas kernels, local(): pl.pallas_call(split_kernel, in_specs=[pl.BlockSpec(memory_space=pltpu.HB...  1.49 us
  transfers between devices with their start and end apart: 20, of which 3 were waited for; matrix products, arithmetic and copies ran while one was open for 1% of the time, Pallas kernels for 28%

profile of v2, /device:TPU:0, one launch (start us, length us, event | category | flops | bytes accessed | tf_op | source)
XLA Modules:
  0.0 63.8 jit_solution(6761538240633754906)
XLA Ops:
  0.6 0.5 collective-permute-start.6
  1.1 0.1 collective-permute-start.7
  1.2 1.5 %shard_map.84 = bf16[4,32,512]{2,1,0:T(8,128)(2,1)} custom-call(bf16[32,2048]{1,0:T(8,128)(2,1)} %grad.1), custom_call_target="tpu_custom_call" | custom-call | tf_op jit(solution)/shard_map/pallas_call | solution.py:394
  2.7 6.3 %all-to-all-start = ((bf16[4,32,512]{2,1,0:T(8,128)(2,1)}), bf16[4,32,512]{2,1,0:T(8,128)(2,1)S(1)}, u32[]{:S(2)}, u32[]{:S(2)}) async-start(bf16[4,32,512]{2,1,0:T(8,128)(2,1)} %shard_map.84), calls=%async_computation | async-start | bytes 262144 | tf_op jit(solution)/shard_map/all_to_all | solution.py:362
  9.0 2.4 %collective-permute-start.2 = (bf16[128,512]{1,0:T(8,128)(2,1)}, bf16[128,512]{1,0:T(8,128)(2,1)S(1)}, u32[]{:S(2)}, u32[]{:S(2)}) collective-permute-start(bf16[128,512]{1,0:T(8,128)(2,1)} %a_1_.3), channel_id=1, source_target_pairs={{0,12},{4,8},{8,4},{12,0},{1,13},{5,9},{9,5},{13,1},{2,14},{6,10},... | collective-permute-start | bytes 393224 | tf_op jit(solution)/shard_map/ppermute | solution.py:339
  11.5 0.5 collective-permute-start.1
  12.0 0.5 collective-permute-start
  12.5 0.7 %pad_add_fusion.a_0_.info = s32[4]{0:T(128)S(1)} fusion(s32[2]{0:T(128)} %param.9, s32[1]{0:T(128)} %bitcast.1, s32[1]{0:T(128)} %bitcast), kind=kLoop, calls=%fused_computation | loop fusion | flops 8 | bytes 32 | tf_op jit(solution)/shard_map/concatenate | solution.py:356
  13.3 2.5 %collective-permute-done.2.a_4_ = bf16[128,512]{1,0:T(8,128)(2,1)S(1)} collective-permute-done((bf16[128,512]{1,0:T(8,128)(2,1)}, bf16[128,512]{1,0:T(8,128)(2,1)S(1)}, u32[]{:S(2)}, u32[]{:S(2)}) %collective-permute-start.2) | collective-permute-done | bytes 131104 | tf_op jit(solution)/shard_map/ppermute | solution.py:339
  15.7 0.0 all-to-all-done
  15.7 3.3 %collective-permute-start.5 = (bf16[128,512]{1,0:T(8,128)(2,1)S(1)}, bf16[128,512]{1,0:T(8,128)(2,1)S(1)}, u32[]{:S(2)}, u32[]{:S(2)}) collective-permute-start(bf16[128,512]{1,0:T(8,128)(2,1)S(1)} %bitcast.4), channel_id=1, source_target_pairs={{0,12},{4,8},{8,4},{12,0},{1,13},{5,9},{9,5},{13,1},{2,14},{6,10},... | collective-permute-start | bytes 393224 | tf_op jit(solution)/shard_map/ppermute | solution.py:339
  19.0 0.0 collective-permute-done.1.a_3_
  19.0 1.0 %collective-permute-start.4 = (bf16[128,512]{1,0:T(8,128)(2,1)S(1)}, bf16[128,512]{1,0:T(8,128)(2,1)S(1)}, u32[]{:S(2)}, u32[]{:S(2)}) collective-permute-start(bf16[128,512]{1,0:T(8,128)(2,1)S(1)} %bitcast.5), channel_id=1, source_target_pairs={{0,8},{4,12},{8,0},{12,4},{1,9},{5,13},{9,1},{13,5},{2,10},{6,14},... | collective-permute-start | bytes 393224 | tf_op jit(solution)/shard_map/ppermute | solution.py:339
  20.0 0.0 collective-permute-done.a_2_
  20.0 0.5 collective-permute-start.3
  20.5 0.0 collective-permute-done.6.a_7_.a_15_
  20.5 0.0 collective-permute-done.7.a_8_.a_16_
  20.5 5.4 %shard_map.85 = (f32[4,2,512]{2,1,0:T(2,128)S(1)}, f32[4,2,512]{2,1,0:T(2,128)S(1)}, f32[512,512]{1,0:T(8,128)S(1)}, bf16[4,4,4,256,256]{4,3,2,1,0:T(8,128)(2,1)S(1)}) custom-call(s32[4]{0:T(128)S(1)} %pad_add_fusion.a_0_.info, bf16[128,512]{1,0:T(8,128)(2,1)} %a_1_.3, bf16[128,512]{1,0:T(8,128)(2,1)S(1)} %collective-permute-done.a_2_, ...), custom_call_target="tpu_custom_call" | custom-call | flops 12884901888 | bytes 1048576 | tf_op jit(solution)/shard_map/pallas_call | solution.py:371
  25.9 0.0 collective-permute-done.5.a_4_.a_8_
  25.9 0.0 collective-permute-done.4.a_3_.a_7_
  25.9 0.0 collective-permute-done.3.a_2_.a_6_
  25.9 0.9 %shard_map.86 = (f32[4,4,512]{2,1,0:T(4,128)S(1)}, bf16[512,128]{1,0:T(8,128)(2,1)S(1)}, bf16[512,128]{1,0:T(8,128)(2,1)S(1)}, bf16[512,128]{1,0:T(8,128)(2,1)S(1)}, bf16[512,128]{1,0:T(8,128)(2,1)S(1)}) custom-call(s32[4]{0:T(128)S(1)} %pad_add_fusion.a_0_.info, bf16[128,512]{1,0:T(8,128)(2,1)S(1)} %bitcast.7, ...), custom_call_target="tpu_custom_call" | custom-call | tf_op jit(solution)/shard_map/pallas_call | solution.py:366
  26.8 2.1 %collective-permute-start.10 = (f32[4,4,512]{2,1,0:T(4,128)S(1)}, f32[4,4,512]{2,1,0:T(4,128)S(1)}, u32[]{:S(2)}, u32[]{:S(2)}) collective-permute-start(f32[4,4,512]{2,1,0:T(4,128)S(1)} %get-tuple-element.43.a_9_.a_5_), channel_id=1, source_target_pairs={{0,12},{4,8},{8,4},{12,0},{1,13},{5,9},{9,5},{13,1},{2,14},{6,10},... | collective-permute-start | bytes 98312 | tf_op jit(solution)/shard_map/ppermute | solution.py:339
  28.9 1.0 %collective-permute-start.9 = (f32[4,4,512]{2,1,0:T(4,128)S(1)}, f32[4,4,512]{2,1,0:T(4,128)S(1)}, u32[]{:S(2)}, u32[]{:S(2)}) collective-permute-start(f32[4,4,512]{2,1,0:T(4,128)S(1)} %get-tuple-element.43.a_9_.a_5_), channel_id=1, source_target_pairs={{0,8},{4,12},{8,0},{12,4},{1,9},{5,13},{9,1},{13,5},{2,10},{6,14},... | collective-permute-start | bytes 98312 | tf_op jit(solution)/shard_map/ppermute | solution.py:339
  29.9 0.5 collective-permute-start.8
  30.4 1.6 %collective-permute-start.11 = (bf16[512,128]{1,0:T(8,128)(2,1)S(1)}, bf16[512,128]{1,0:T(8,128)(2,1)S(1)}, u32[]{:S(2)}, u32[]{:S(2)}) collective-permute-start(bf16[512,128]{1,0:T(8,128)(2,1)S(1)} %get-tuple-element.54), channel_id=1, source_target_pairs={{0,4},{4,0},{8,12},{12,8},{1,5},{5,1},{9,13},{13,9},{2,6},{6,2},{1... | collective-permute-start | bytes 393224 | tf_op jit(solution)/shard_map/ppermute | solution.py:339
  31.9 1.0 %collective-permute-start.12 = (bf16[512,128]{1,0:T(8,128)(2,1)S(1)}, bf16[512,128]{1,0:T(8,128)(2,1)S(1)}, u32[]{:S(2)}, u32[]{:S(2)}) collective-permute-start(bf16[512,128]{1,0:T(8,128)(2,1)S(1)} %get-tuple-element.55), channel_id=1, source_target_pairs={{0,8},{4,12},{8,0},{12,4},{1,9},{5,13},{9,1},{13,5},{2,10},{6,14},... | collective-permute-start | bytes 393224 | tf_op jit(solution)/shard_map/ppermute | solution.py:339
  33.0 0.0 collective-permute-done.10.a_12_.a_8_
  33.0 0.9 %collective-permute-start.13 = (bf16[512,128]{1,0:T(8,128)(2,1)S(1)}, bf16[512,128]{1,0:T(8,128)(2,1)S(1)}, u32[]{:S(2)}, u32[]{:S(2)}) collective-permute-start(bf16[512,128]{1,0:T(8,128)(2,1)S(1)} %get-tuple-element.56), channel_id=1, source_target_pairs={{0,12},{4,8},{8,4},{12,0},{1,13},{5,9},{9,5},{13,1},{2,14},{6,10},... | collective-permute-start | bytes 393224 | tf_op jit(solution)/shard_map/ppermute | solution.py:339
  33.9 0.0 collective-permute-done.9.a_11_.a_7_
  33.9 0.0 collective-permute-done.8.a_10_.a_6_
  33.9 1.2 %copy-done.1 = bf16[2,512,512]{2,1,0:T(8,128)(2,1)S(1)} copy-done((bf16[2,512,512]{2,1,0:T(8,128)(2,1)S(1)}, bf16[2,512,512]{2,1,0:T(8,128)(2,1)}, u32[]{:S(2)}) %copy-start.1) | copy-done | bytes 1048600
  35.1 8.0 %shard_map.87 = (bf16[2,512,512]{2,1,0:T(8,128)(2,1)}, bf16[2,512,512]{2,1,0:T(8,128)(2,1)}, bf16[2,512,512]{2,1,0:T(8,128)(2,1)}, bf16[512,128]{1,0:T(8,128)(2,...) custom-call(s32[4]{0:T(128)S(1)} %pad_add_fusion.a_0_.info, ...), custom_call_target="tpu_custom_call" | custom-call | flops 25769803776 | bytes 1048576 | tf_op jit(solution)/shard_map/pallas_call | solution.py:371
  43.1 0.0 collective-permute-done.11.a_2_
  43.1 0.0 collective-permute-done.12.a_3_
  43.1 0.0 collective-permute-done.13.a_4_
  43.1 5.0 %collective-permute-start.17 = (bf16[2,512,512]{2,1,0:T(8,128)(2,1)}, bf16[2,512,512]{2,1,0:T(8,128)(2,1)S(1)}, u32[]{:S(2)}, u32[]{:S(2)}) collective-permute-start(bf16[2,512,512]{2,1,0:T(8,128)(2,1)} %get-tuple-element.61), channel_id=1, source_target_pairs={{0,16},{16,0},{1,17},{17,1},{2,18},{18,2},{3,19},{19,3},{4,20},{20... | collective-permute-start | bytes 3145736 | tf_op jit(solution)/shard_map/ppermute | solution.py:339
  48.1 1.4 %shard_map.89 = bf16[128,512]{1,0:T(8,128)(2,1)} custom-call(s32[4]{0:T(128)S(1)} %pad_add_fusion.a_0_.info, bf16[512,128]{1,0:T(8,128)(2,1)S(1)} %get-tuple-element.70.a_1_, bf16[512,128]{1,0:T(8,128)(2,1)S(1)} %collective-permute-done.11.a_2_, bf16[512,128]{1,0:T(8,128)(2,1)S(1)} %collective-permute-done.12.a_3_, ...), custom_call_target="tpu_custom_call" | custom-call | tf_op jit(solution)/shard_map/pallas_call | solution.py:366
  49.5 4.7 %all-to-all-start.1 = ((bf16[4,32,512]{2,1,0:T(8,128)(2,1)}), bf16[4,32,512]{2,1,0:T(8,128)(2,1)S(1)}, u32[]{:S(2)}, u32[]{:S(2)}) async-start(bf16[4,32,512]{2,1,0:T(8,128)(2,1)} %bitcast.3), calls=%async_computation.1 | async-start | bytes 262144 | tf_op jit(solution)/shard_map/all_to_all | solution.py:362
  54.2 1.1 %collective-permute-start.14 = (bf16[512,128]{1,0:T(8,128)(2,1)S(1)}, bf16[512,128]{1,0:T(8,128)(2,1)S(1)}, u32[]{:S(2)}, u32[]{:S(2)}) collective-permute-start(bf16[512,128]{1,0:T(8,128)(2,1)S(1)} %get-tuple-element.58), channel_id=1, source_target_pairs={{0,4},{4,0},{8,12},{12,8},{1,5},{5,1},{9,13},{13,9},{2,6},{6,2},{1... | collective-permute-start | bytes 393224 | tf_op jit(solution)/shard_map/ppermute | solution.py:339
  55.3 0.6 %collective-permute-start.15 = (bf16[512,128]{1,0:T(8,128)(2,1)S(1)}, bf16[512,128]{1,0:T(8,128)(2,1)S(1)}, u32[]{:S(2)}, u32[]{:S(2)}) collective-permute-start(bf16[512,128]{1,0:T(8,128)(2,1)S(1)} %get-tuple-element.59), channel_id=1, source_target_pairs={{0,8},{4,12},{8,0},{12,4},{1,9},{5,13},{9,1},{13,5},{2,10},{6,14},... | collective-permute-start | bytes 393224 | tf_op jit(solution)/shard_map/ppermute | solution.py:339
  55.9 1.8 %collective-permute-start.16 = (bf16[512,128]{1,0:T(8,128)(2,1)S(1)}, bf16[512,128]{1,0:T(8,128)(2,1)S(1)}, u32[]{:S(2)}, u32[]{:S(2)}) collective-permute-start(bf16[512,128]{1,0:T(8,128)(2,1)S(1)} %get-tuple-element.60), channel_id=1, source_target_pairs={{0,12},{4,8},{8,4},{12,0},{1,13},{5,9},{9,5},{13,1},{2,14},{6,10},... | collective-permute-start | bytes 393224 | tf_op jit(solution)/shard_map/ppermute | solution.py:339
  57.7 1.7 %shard_map.88 = (bf16[2,512,512]{2,1,0:T(8,128)(2,1)}, bf16[2,512,512]{2,1,0:T(8,128)(2,1)}) custom-call(s32[4]{0:T(128)S(1)} %pad_add_fusion.a_0_.info, bf16[2,512,512]{2,1,0:T(8,128)(2,1)S(1)} %collective-permute-done.17.back, bf16[2,512,512]{2,1,0:T(8,128)(2,1)} %get-tuple-element.62.dk_in, ...), custom_call_target="tpu_custom_call", output_to_operand_aliasing={{0}: (2, {}), {1}: (3, {})} | custom-call | bytes 1048576 | tf_op jit(solution)/shard_map/pallas_call | solution.py:371
  59.3 0.8 %collective-permute-done.14.a_1_ = bf16[512,128]{1,0:T(8,128)(2,1)S(1)} collective-permute-done((bf16[512,128]{1,0:T(8,128)(2,1)S(1)}, bf16[512,128]{1,0:T(8,128)(2,1)S(1)}, u32[]{:S(2)}, u32[]{:S(2)}) %collective-permute-start.14) | collective-permute-done | bytes 131104 | tf_op jit(solution)/shard_map/ppermute | solution.py:339
  60.2 2.8 %collective-permute-done.15.a_2_ = bf16[512,128]{1,0:T(8,128)(2,1)S(1)} collective-permute-done((bf16[512,128]{1,0:T(8,128)(2,1)S(1)}, bf16[512,128]{1,0:T(8,128)(2,1)S(1)}, u32[]{:S(2)}, u32[]{:S(2)}) %collective-permute-start.15) | collective-permute-done | bytes 131104 | tf_op jit(solution)/shard_map/ppermute | solution.py:339
  62.9 0.0 collective-permute-done.16.a_3_
  63.0 0.0 all-to-all-done.1.a_4_
  63.0 0.8 %shard_map.90 = (bf16[128,512]{1,0:T(8,128)(2,1)}, bf16[32,2048]{1,0:T(8,128)(2,1)}) custom-call(bf16[512,128]{1,0:T(8,128)(2,1)S(1)} %get-tuple-element.66.a_0_, bf16[512,128]{1,0:T(8,128)(2,1)S(1)} %collective-permute-done.14.a_1_, bf16[512,128]{1,0:T(8,128)(2,1)S(1)} %collective-permute-done.15.a_2_, bf16[512,128]{1,0:T(8,128)(2,1)S(1)} %collective-permute-done.16.a_3_, ...), custom_call_target="tpu_custom_call" | custom-call | tf_op jit(solution)/shard_map/pallas_call | solution.py:366
  (4 shorter events, 0.0 us)
Async XLA Ops:
  0.6 19.8 %collective-permute-start.6 = (bf16[2,512,512]{2,1,0:T(8,128)(2,1)}, bf16[2,512,512]{2,1,0:T(8,128)(2,1)S(1)}, u32[]{:S(2)}, u32[]{:S(2)}) collective-permute-start(bf16[2,512,512]{2,1,0:T(8,128)(2,1)} %a_13_.1), channel_id=1, source_target_pairs={{0,16},{16,0},{1,17},{17,1},{2,18},{18,2},{3,19},{19,3},{4,20},{20... | collective-permute-start | bytes 3145736 | tf_op jit(solution)/shard_map/ppermute | solution.py:339
  1.1 19.3 %collective-permute-start.7 = (bf16[2,512,512]{2,1,0:T(8,128)(2,1)}, bf16[2,512,512]{2,1,0:T(8,128)(2,1)S(1)}, u32[]{:S(2)}, u32[]{:S(2)}) collective-permute-start(bf16[2,512,512]{2,1,0:T(8,128)(2,1)} %a_14_.1), channel_id=1, source_target_pairs={{0,16},{16,0},{1,17},{17,1},{2,18},{18,2},{3,19},{19,3},{4,20},{20... | collective-permute-start | bytes 3145736 | tf_op jit(solution)/shard_map/ppermute | solution.py:339
  2.7 13.0 %all-to-all-start = ((bf16[4,32,512]{2,1,0:T(8,128)(2,1)}), bf16[4,32,512]{2,1,0:T(8,128)(2,1)S(1)}, u32[]{:S(2)}, u32[]{:S(2)}) async-start(bf16[4,32,512]{2,1,0:T(8,128)(2,1)} %shard_map.84), calls=%async_computation | async-start | bytes 262144 | tf_op jit(solution)/shard_map/all_to_all | solution.py:362
  9.0 6.7 %collective-permute-start.2 = (bf16[128,512]{1,0:T(8,128)(2,1)}, bf16[128,512]{1,0:T(8,128)(2,1)S(1)}, u32[]{:S(2)}, u32[]{:S(2)}) collective-permute-start(bf16[128,512]{1,0:T(8,128)(2,1)} %a_1_.3), channel_id=1, source_target_pairs={{0,12},{4,8},{8,4},{12,0},{1,13},{5,9},{9,5},{13,1},{2,14},{6,10},... | collective-permute-start | bytes 393224 | tf_op jit(solution)/shard_map/ppermute | solution.py:339
  11.5 7.5 %collective-permute-start.1 = (bf16[128,512]{1,0:T(8,128)(2,1)}, bf16[128,512]{1,0:T(8,128)(2,1)S(1)}, u32[]{:S(2)}, u32[]{:S(2)}) collective-permute-start(bf16[128,512]{1,0:T(8,128)(2,1)} %a_1_.3), channel_id=1, source_target_pairs={{0,8},{4,12},{8,0},{12,4},{1,9},{5,13},{9,1},{13,5},{2,10},{6,14},... | collective-permute-start | bytes 393224 | tf_op jit(solution)/shard_map/ppermute | solution.py:339
  12.0 8.0 %collective-permute-start = (bf16[128,512]{1,0:T(8,128)(2,1)}, bf16[128,512]{1,0:T(8,128)(2,1)S(1)}, u32[]{:S(2)}, u32[]{:S(2)}) collective-permute-start(bf16[128,512]{1,0:T(8,128)(2,1)} %a_1_.3), channel_id=1, source_target_pairs={{0,4},{4,0},{8,12},{12,8},{1,5},{5,1},{9,13},{13,9},{2,6},{6,2},{1... | collective-permute-start | bytes 393224 | tf_op jit(solution)/shard_map/ppermute | solution.py:339
  15.7 10.2 %collective-permute-start.5 = (bf16[128,512]{1,0:T(8,128)(2,1)S(1)}, bf16[128,512]{1,0:T(8,128)(2,1)S(1)}, u32[]{:S(2)}, u32[]{:S(2)}) collective-permute-start(bf16[128,512]{1,0:T(8,128)(2,1)S(1)} %bitcast.4), channel_id=1, source_target_pairs={{0,12},{4,8},{8,4},{12,0},{1,13},{5,9},{9,5},{13,1},{2,14},{6,10},... | collective-permute-start | bytes 393224 | tf_op jit(solution)/shard_map/ppermute | solution.py:339
  19.0 6.9 %collective-permute-start.4 = (bf16[128,512]{1,0:T(8,128)(2,1)S(1)}, bf16[128,512]{1,0:T(8,128)(2,1)S(1)}, u32[]{:S(2)}, u32[]{:S(2)}) collective-permute-start(bf16[128,512]{1,0:T(8,128)(2,1)S(1)} %bitcast.5), channel_id=1, source_target_pairs={{0,8},{4,12},{8,0},{12,4},{1,9},{5,13},{9,1},{13,5},{2,10},{6,14},... | collective-permute-start | bytes 393224 | tf_op jit(solution)/shard_map/ppermute | solution.py:339
  20.0 5.9 %collective-permute-start.3 = (bf16[128,512]{1,0:T(8,128)(2,1)S(1)}, bf16[128,512]{1,0:T(8,128)(2,1)S(1)}, u32[]{:S(2)}, u32[]{:S(2)}) collective-permute-start(bf16[128,512]{1,0:T(8,128)(2,1)S(1)} %bitcast.6), channel_id=1, source_target_pairs={{0,4},{4,0},{8,12},{12,8},{1,5},{5,1},{9,13},{13,9},{2,6},{6,2},{1... | collective-permute-start | bytes 393224 | tf_op jit(solution)/shard_map/ppermute | solution.py:339
  20.5 5.4 %copy-start = (bf16[2,512,512]{2,1,0:T(8,128)(2,1)}, bf16[2,512,512]{2,1,0:T(8,128)(2,1)S(1)}, u32[]{:S(2)}) copy-start(bf16[2,512,512]{2,1,0:T(8,128)(2,1)S(1)} %collective-permute-done.7.a_8_.a_16_) | copy-start | bytes 3145732
  26.8 6.1 %collective-permute-start.10 = (f32[4,4,512]{2,1,0:T(4,128)S(1)}, f32[4,4,512]{2,1,0:T(4,128)S(1)}, u32[]{:S(2)}, u32[]{:S(2)}) collective-permute-start(f32[4,4,512]{2,1,0:T(4,128)S(1)} %get-tuple-element.43.a_9_.a_5_), channel_id=1, source_target_pairs={{0,12},{4,8},{8,4},{12,0},{1,13},{5,9},{9,5},{13,1},{2,14},{6,10},... | collective-permute-start | bytes 98312 | tf_op jit(solution)/shard_map/ppermute | solution.py:339
  28.9 5.0 %collective-permute-start.9 = (f32[4,4,512]{2,1,0:T(4,128)S(1)}, f32[4,4,512]{2,1,0:T(4,128)S(1)}, u32[]{:S(2)}, u32[]{:S(2)}) collective-permute-start(f32[4,4,512]{2,1,0:T(4,128)S(1)} %get-tuple-element.43.a_9_.a_5_), channel_id=1, source_target_pairs={{0,8},{4,12},{8,0},{12,4},{1,9},{5,13},{9,1},{13,5},{2,10},{6,14},... | collective-permute-start | bytes 98312 | tf_op jit(solution)/shard_map/ppermute | solution.py:339
  29.9 4.0 %collective-permute-start.8 = (f32[4,4,512]{2,1,0:T(4,128)S(1)}, f32[4,4,512]{2,1,0:T(4,128)S(1)}, u32[]{:S(2)}, u32[]{:S(2)}) collective-permute-start(f32[4,4,512]{2,1,0:T(4,128)S(1)} %get-tuple-element.43.a_9_.a_5_), channel_id=1, source_target_pairs={{0,4},{4,0},{8,12},{12,8},{1,5},{5,1},{9,13},{13,9},{2,6},{6,2},{1... | collective-permute-start | bytes 98312 | tf_op jit(solution)/shard_map/ppermute | solution.py:339
  30.4 12.7 %collective-permute-start.11 = (bf16[512,128]{1,0:T(8,128)(2,1)S(1)}, bf16[512,128]{1,0:T(8,128)(2,1)S(1)}, u32[]{:S(2)}, u32[]{:S(2)}) collective-permute-start(bf16[512,128]{1,0:T(8,128)(2,1)S(1)} %get-tuple-element.54), channel_id=1, source_target_pairs={{0,4},{4,0},{8,12},{12,8},{1,5},{5,1},{9,13},{13,9},{2,6},{6,2},{1... | collective-permute-start | bytes 393224 | tf_op jit(solution)/shard_map/ppermute | solution.py:339
  31.9 11.1 %collective-permute-start.12 = (bf16[512,128]{1,0:T(8,128)(2,1)S(1)}, bf16[512,128]{1,0:T(8,128)(2,1)S(1)}, u32[]{:S(2)}, u32[]{:S(2)}) collective-permute-start(bf16[512,128]{1,0:T(8,128)(2,1)S(1)} %get-tuple-element.55), channel_id=1, source_target_pairs={{0,8},{4,12},{8,0},{12,4},{1,9},{5,13},{9,1},{13,5},{2,10},{6,14},... | collective-permute-start | bytes 393224 | tf_op jit(solution)/shard_map/ppermute | solution.py:339
  33.0 10.1 %collective-permute-start.13 = (bf16[512,128]{1,0:T(8,128)(2,1)S(1)}, bf16[512,128]{1,0:T(8,128)(2,1)S(1)}, u32[]{:S(2)}, u32[]{:S(2)}) collective-permute-start(bf16[512,128]{1,0:T(8,128)(2,1)S(1)} %get-tuple-element.56), channel_id=1, source_target_pairs={{0,12},{4,8},{8,4},{12,0},{1,13},{5,9},{9,5},{13,1},{2,14},{6,10},... | collective-permute-start | bytes 393224 | tf_op jit(solution)/shard_map/ppermute | solution.py:339
  33.9 1.2 %copy-start.1 = (bf16[2,512,512]{2,1,0:T(8,128)(2,1)S(1)}, bf16[2,512,512]{2,1,0:T(8,128)(2,1)}, u32[]{:S(2)}) copy-start(bf16[2,512,512]{2,1,0:T(8,128)(2,1)} %copy-done) | copy-start | bytes 3145732
  43.1 14.6 %collective-permute-start.17 = (bf16[2,512,512]{2,1,0:T(8,128)(2,1)}, bf16[2,512,512]{2,1,0:T(8,128)(2,1)S(1)}, u32[]{:S(2)}, u32[]{:S(2)}) collective-permute-start(bf16[2,512,512]{2,1,0:T(8,128)(2,1)} %get-tuple-element.61), channel_id=1, source_target_pairs={{0,16},{16,0},{1,17},{17,1},{2,18},{18,2},{3,19},{19,3},{4,20},{20... | collective-permute-start | bytes 3145736 | tf_op jit(solution)/shard_map/ppermute | solution.py:339
  49.5 13.5 %all-to-all-start.1 = ((bf16[4,32,512]{2,1,0:T(8,128)(2,1)}), bf16[4,32,512]{2,1,0:T(8,128)(2,1)S(1)}, u32[]{:S(2)}, u32[]{:S(2)}) async-start(bf16[4,32,512]{2,1,0:T(8,128)(2,1)} %bitcast.3), calls=%async_computation.1 | async-start | bytes 262144 | tf_op jit(solution)/shard_map/all_to_all | solution.py:362
  54.2 6.0 %collective-permute-start.14 = (bf16[512,128]{1,0:T(8,128)(2,1)S(1)}, bf16[512,128]{1,0:T(8,128)(2,1)S(1)}, u32[]{:S(2)}, u32[]{:S(2)}) collective-permute-start(bf16[512,128]{1,0:T(8,128)(2,1)S(1)} %get-tuple-element.58), channel_id=1, source_target_pairs={{0,4},{4,0},{8,12},{12,8},{1,5},{5,1},{9,13},{13,9},{2,6},{6,2},{1... | collective-permute-start | bytes 393224 | tf_op jit(solution)/shard_map/ppermute | solution.py:339
  55.3 7.7 %collective-permute-start.15 = (bf16[512,128]{1,0:T(8,128)(2,1)S(1)}, bf16[512,128]{1,0:T(8,128)(2,1)S(1)}, u32[]{:S(2)}, u32[]{:S(2)}) collective-permute-start(bf16[512,128]{1,0:T(8,128)(2,1)S(1)} %get-tuple-element.59), channel_id=1, source_target_pairs={{0,8},{4,12},{8,0},{12,4},{1,9},{5,13},{9,1},{13,5},{2,10},{6,14},... | collective-permute-start | bytes 393224 | tf_op jit(solution)/shard_map/ppermute | solution.py:339
  55.9 7.0 %collective-permute-start.16 = (bf16[512,128]{1,0:T(8,128)(2,1)S(1)}, bf16[512,128]{1,0:T(8,128)(2,1)S(1)}, u32[]{:S(2)}, u32[]{:S(2)}) collective-permute-start(bf16[512,128]{1,0:T(8,128)(2,1)S(1)} %get-tuple-element.60), channel_id=1, source_target_pairs={{0,12},{4,8},{8,4},{12,0},{1,13},{5,9},{9,5},{13,1},{2,14},{6,10},... | collective-permute-start | bytes 393224 | tf_op jit(solution)/shard_map/ppermute | solution.py:339

commit v3 on v2

--- a/solution.py
+++ b/solution.py
@@ -91,7 +91,7 @@
 
 def forward_kernel(n, rows, info, *refs):
     q = refs[:n]
-    k_own, v_own, k_oth, v_oth, lse_ref, top_ref, out_ref, exp_ref = refs[n:]
+    k_own, v_own, k_oth, v_oth, lse_ref, top_ref, out_ref, exp_ref, kt_ref, v_ref = refs[n:]
     first_pair = pl.program_id(0) * lse_ref.shape[0]
 
     def run(blocks, rest):
@@ -102,7 +102,11 @@
         for p in range(lse_ref.shape[0]):
             lanes = slice(p * PAIR, (p + 1) * PAIR)
             ks[p] = sources(k_own, k_oth, lanes)
-            vt = [x.T for x in sources(v_own, v_oth, lanes)]
+            vs = sources(v_own, v_oth, lanes)
+            vt = [x.T for x in vs]
+            for c in range(len(vs)):
+                kt_ref[first_pair + p, c] = ks[p][c].T
+                v_ref[first_pair + p, c] = vs[c]
             row = lax.broadcasted_iota(jnp.int32, (16, vt[0].shape[1]), 0)
             ones = (row == 0).astype(F32).astype(BF16)
             for u in range(2):
@@ -186,9 +190,9 @@
 
 def backward_kernel(n, rows, info, *refs):
     q, g, stats = refs[:n], refs[n : 2 * n], refs[2 * n : 3 * n]
-    k_own, v_own, k_oth, v_oth, top_ref, exp_ref = refs[3 * n : 3 * n + 6]
-    dk_own, dv_own, d_oth = refs[3 * n + 6 : 3 * n + 9]
-    dq = refs[3 * n + 9 :]
+    top_ref, exp_ref, kt_ref, v_ref = refs[3 * n : 3 * n + 4]
+    dk_own, dv_own, d_oth = refs[3 * n + 4 : 3 * n + 7]
+    dq = refs[3 * n + 7 :]
     first_pair = pl.program_id(0) * top_ref.shape[0]
     scale = 1.0 / math.sqrt(HEAD_DIM)
 
@@ -199,15 +203,13 @@
         return jnp.concatenate([line[:, (k ^ j) * rows : ((k ^ j) + 1) * rows] for k in slots], axis=1)
 
     def run(blocks, rest):
-        def sources(own, oth, lanes):
-            return chunked([own[0, :, lanes], oth[0, :, lanes]])
-
         vs, kt, operands = {}, {}, {}
         pairs = stats[0].shape[0]
         for p in range(pairs):
             lanes = slice(p * PAIR, (p + 1) * PAIR)
-            vs[p] = [with_ones(x) for x in sources(v_own, v_oth, lanes)]
-            kt[p] = [x.T for x in sources(k_own, k_oth, lanes)]
+            chunks = range(v_ref.shape[1])
+            vs[p] = [with_ones(v_ref[first_pair + p, c]) for c in chunks]
+            kt[p] = [kt_ref[first_pair + p, c] for c in chunks]
             for b, slots in enumerate(blocks):
                 qb = stack_slots(q, slots, lanes) * lane_scale()
                 gb = slot_cotangents(g, info, n, slots, lanes)
@@ -403,11 +405,14 @@
     flop = 24 * tgt * 2 * src * width
     chunk, per = min(256, src), rows * len(target_blocks(n, rows)[0])
     exps = (pairs, 2 * (tgt // per), 2 * src // chunk, chunk, per)
-    lse, top, out_t, exps = call(
+    count = 2 * src // chunk
+    lse, top, out_t, exps, kt, v = call(
         lambda *a: forward_kernel(n, rows, *a),
         slot_in + [own] * 4,
-        [lse_spec, lse_spec, out_spec, whole],
-        [sds((pairs, 2, tgt), F32)] * 2 + [sds((width, tgt), F32), sds(exps, BF16)],
+        [lse_spec, lse_spec, out_spec, whole, whole, whole],
+        [sds((pairs, 2, tgt), F32)] * 2
+        + [sds((width, tgt), F32), sds(exps, BF16)]
+        + [sds((pairs, count, PAIR, chunk), BF16), sds((pairs, count, chunk, PAIR), BF16)],
         [stay(queries), *q[1:], stay(keys), stay(values), k_oth, v_oth],
         flops=2 * flop,
     )
@@ -427,10 +432,10 @@
     outs = [sends[0]] + [xor_permute(sends[k], "seq", n, k) for k in range(1, n)]
     grads = call(
         lambda *a: backward_kernel(n, rows, *a),
-        slot_in + slot_in + [stats_spec] * n + [own] * 4 + [lse_spec, whole],
+        slot_in + slot_in + [stats_spec] * n + [lse_spec, whole, whole, whole],
         [own, own, oth] + slot_t,
         [sds((2, src, width), BF16)] * 3 + [sds((width, rows), BF16)] * n,
-        [stay(queries), *q[1:], *g, *all_stats, stay(keys), stay(values), k_oth, v_oth, top, exps],
+        [stay(queries), *q[1:], *g, *all_stats, top, exps, kt, v],
         flops=4 * flop,
     )
     (dk, dv, d_oth, *dq), outs = lax.optimization_barrier((grads, outs))

time: 62.5 us -> 66 us (1.056); the launches traced: 63.8 us -> 65.5 us
  Pallas kernels: 19.6 us -> 26.1 us
  starting transfers between devices: 35.4 us -> 30.9 us
  local copies, waits for them, and re-layouts: 1.23 us -> 0 us
  waiting for transfers between devices: 6.1 us -> 7.09 us
    pallas_call x3, Pallas kernels: 15 us -> 21.4 us  [call(): pl.pallas_call(kernel, grid_spec=pltpu.PrefetchScalarGridSpec(num_scalar_...]
    ppermute x18, starting transfers between devices: 24.3 us -> 19.8 us  [xor_permute(): return lax.ppermute(x, axis, [(i, i ^ k) for i in range(size)])]
    unnamed x4 -> x0, local copies, waits for them, and re-layouts: 1.23 us -> none
    ppermute x18, waiting for transfers between devices: 6.1 us -> 7.09 us  [xor_permute(): return lax.ppermute(x, axis, [(i, i ^ k) for i in range(size)])]
  transfers between devices with their start and end apart: 20 -> 20, of which waited for: 3 -> 3; matrix products, arithmetic and copies ran while one was open for 1% -> 1% of each run, Pallas kernels for 28% -> 37%
where the time goes in v3:
time: 66 us; the launch traced here: 65.5 us
  starting transfers between devices  30.9 us (47%)
  Pallas kernels  26.1 us (40%)
  waiting for transfers between devices  7.09 us (11%)
  other arithmetic  0.73 us (1%)
  between operations  0.72 us (1%)
    pallas_call x3, Pallas kernels, call(): pl.pallas_call(kernel, grid_spec=pltpu.PrefetchScalarGridSpec(num_scalar_...  21.4 us
    ppermute x18, starting transfers between devices, xor_permute(): return lax.ppermute(x, axis, [(i, i ^ k) for i in range(size)])  19.8 us
    all_to_all x2, starting transfers between devices, exchange(): return lax.all_to_all(x, 'head', split_axis=0, concat_axis=0, tiled=True)  11.1 us
    ppermute x18, waiting for transfers between devices, xor_permute(): return lax.ppermute(x, axis, [(i, i ^ k) for i in range(size)])  7.09 us
    pallas_call x3, Pallas kernels, plain(): pl.pallas_call(kernel, in_specs=in_specs, out_specs=out_specs, out_shape=...  3.13 us
    pallas_call x1, Pallas kernels, local(): pl.pallas_call(split_kernel, in_specs=[pl.BlockSpec(memory_space=pltpu.HB...  1.49 us
  transfers between devices with their start and end apart: 20, of which 3 were waited for; matrix products, arithmetic and copies ran while one was open for 1% of the time, Pallas kernels for 37%

profile of v3, /device:TPU:0, one launch (start us, length us, event | category | flops | bytes accessed | tf_op | source)
XLA Modules:
  0.0 65.5 jit_solution(13501541241108491088)
XLA Ops:
  0.6 0.5 collective-permute-start.6
  1.1 0.1 collective-permute-start.7
  1.2 1.5 %shard_map.84 = bf16[4,32,512]{2,1,0:T(8,128)(2,1)} custom-call(bf16[32,2048]{1,0:T(8,128)(2,1)} %grad.1), custom_call_target="tpu_custom_call" | custom-call | tf_op jit(solution)/shard_map/pallas_call | solution.py:396
  2.7 6.3 %all-to-all-start = ((bf16[4,32,512]{2,1,0:T(8,128)(2,1)}), bf16[4,32,512]{2,1,0:T(8,128)(2,1)S(1)}, u32[]{:S(2)}, u32[]{:S(2)}) async-start(bf16[4,32,512]{2,1,0:T(8,128)(2,1)} %shard_map.84), calls=%async_computation | async-start | bytes 262144 | tf_op jit(solution)/shard_map/all_to_all | solution.py:364
  9.0 2.4 %collective-permute-start.2 = (bf16[128,512]{1,0:T(8,128)(2,1)}, bf16[128,512]{1,0:T(8,128)(2,1)S(1)}, u32[]{:S(2)}, u32[]{:S(2)}) collective-permute-start(bf16[128,512]{1,0:T(8,128)(2,1)} %a_1_.3), channel_id=1, source_target_pairs={{0,12},{4,8},{8,4},{12,0},{1,13},{5,9},{9,5},{13,1},{2,14},{6,10},... | collective-permute-start | bytes 393224 | tf_op jit(solution)/shard_map/ppermute | solution.py:341
  11.5 0.5 collective-permute-start.1
  12.0 0.5 collective-permute-start
  12.5 0.7 %pad_add_fusion.a_0_.info = s32[4]{0:T(128)S(1)} fusion(s32[2]{0:T(128)} %param.9, s32[1]{0:T(128)} %bitcast.1, s32[1]{0:T(128)} %bitcast), kind=kLoop, calls=%fused_computation | loop fusion | flops 8 | bytes 32 | tf_op jit(solution)/shard_map/concatenate | solution.py:358
  13.3 2.5 %collective-permute-done.2.a_4_ = bf16[128,512]{1,0:T(8,128)(2,1)S(1)} collective-permute-done((bf16[128,512]{1,0:T(8,128)(2,1)}, bf16[128,512]{1,0:T(8,128)(2,1)S(1)}, u32[]{:S(2)}, u32[]{:S(2)}) %collective-permute-start.2) | collective-permute-done | bytes 131104 | tf_op jit(solution)/shard_map/ppermute | solution.py:341
  15.7 0.0 all-to-all-done
  15.7 3.3 %collective-permute-start.5 = (bf16[128,512]{1,0:T(8,128)(2,1)S(1)}, bf16[128,512]{1,0:T(8,128)(2,1)S(1)}, u32[]{:S(2)}, u32[]{:S(2)}) collective-permute-start(bf16[128,512]{1,0:T(8,128)(2,1)S(1)} %bitcast.4), channel_id=1, source_target_pairs={{0,12},{4,8},{8,4},{12,0},{1,13},{5,9},{9,5},{13,1},{2,14},{6,10},... | collective-permute-start | bytes 393224 | tf_op jit(solution)/shard_map/ppermute | solution.py:341
  19.0 0.0 collective-permute-done.1.a_3_
  19.0 1.0 %collective-permute-start.4 = (bf16[128,512]{1,0:T(8,128)(2,1)S(1)}, bf16[128,512]{1,0:T(8,128)(2,1)S(1)}, u32[]{:S(2)}, u32[]{:S(2)}) collective-permute-start(bf16[128,512]{1,0:T(8,128)(2,1)S(1)} %bitcast.5), channel_id=1, source_target_pairs={{0,8},{4,12},{8,0},{12,4},{1,9},{5,13},{9,1},{13,5},{2,10},{6,14},... | collective-permute-start | bytes 393224 | tf_op jit(solution)/shard_map/ppermute | solution.py:341
  20.0 0.0 collective-permute-done.a_2_
  20.0 0.5 collective-permute-start.3
  20.5 0.0 collective-permute-done.6.a_7_
  20.5 0.0 collective-permute-done.7.a_8_
  20.5 8.6 %shard_map.85 = (f32[4,2,512]{2,1,0:T(2,128)S(1)}, f32[4,2,512]{2,1,0:T(2,128)S(1)}, f32[512,512]{1,0:T(8,128)S(1)}, bf16[4,4,4,256,256]{4,3,2,1,0:T(8,128)(2,1)...) custom-call(s32[4]{0:T(128)S(1)} %pad_add_fusion.a_0_.info, bf16[128,512]{1,0:T(8,128)(2,1)} %a_1_.3, ...), custom_call_target="tpu_custom_call" | custom-call | flops 12884901888 | bytes 1048576 | tf_op jit(solution)/shard_map/pallas_call | solution.py:373
  29.1 0.0 collective-permute-done.5.a_4_.a_8_
  29.1 0.0 collective-permute-done.4.a_3_.a_7_
  29.1 0.0 collective-permute-done.3.a_2_.a_6_
  29.1 0.9 %shard_map.86 = (f32[4,4,512]{2,1,0:T(4,128)S(1)}, bf16[512,128]{1,0:T(8,128)(2,1)S(1)}, bf16[512,128]{1,0:T(8,128)(2,1)S(1)}, bf16[512,128]{1,0:T(8,128)(2,1)S(1)}, bf16[512,128]{1,0:T(8,128)(2,1)S(1)}) custom-call(s32[4]{0:T(128)S(1)} %pad_add_fusion.a_0_.info, bf16[128,512]{1,0:T(8,128)(2,1)S(1)} %bitcast.7, ...), custom_call_target="tpu_custom_call" | custom-call | tf_op jit(solution)/shard_map/pallas_call | solution.py:368
  30.0 2.1 %collective-permute-start.10 = (f32[4,4,512]{2,1,0:T(4,128)S(1)}, f32[4,4,512]{2,1,0:T(4,128)S(1)}, u32[]{:S(2)}, u32[]{:S(2)}) collective-permute-start(f32[4,4,512]{2,1,0:T(4,128)S(1)} %get-tuple-element.45.a_9_.a_5_), channel_id=1, source_target_pairs={{0,12},{4,8},{8,4},{12,0},{1,13},{5,9},{9,5},{13,1},{2,14},{6,10},... | collective-permute-start | bytes 98312 | tf_op jit(solution)/shard_map/ppermute | solution.py:341
  32.1 1.0 %collective-permute-start.9 = (f32[4,4,512]{2,1,0:T(4,128)S(1)}, f32[4,4,512]{2,1,0:T(4,128)S(1)}, u32[]{:S(2)}, u32[]{:S(2)}) collective-permute-start(f32[4,4,512]{2,1,0:T(4,128)S(1)} %get-tuple-element.45.a_9_.a_5_), channel_id=1, source_target_pairs={{0,8},{4,12},{8,0},{12,4},{1,9},{5,13},{9,1},{13,5},{2,10},{6,14},... | collective-permute-start | bytes 98312 | tf_op jit(solution)/shard_map/ppermute | solution.py:341
  33.1 0.5 collective-permute-start.8
  33.6 1.5 %collective-permute-start.11 = (bf16[512,128]{1,0:T(8,128)(2,1)S(1)}, bf16[512,128]{1,0:T(8,128)(2,1)S(1)}, u32[]{:S(2)}, u32[]{:S(2)}) collective-permute-start(bf16[512,128]{1,0:T(8,128)(2,1)S(1)} %get-tuple-element.58), channel_id=1, source_target_pairs={{0,4},{4,0},{8,12},{12,8},{1,5},{5,1},{9,13},{13,9},{2,6},{6,2},{1... | collective-permute-start | bytes 393224 | tf_op jit(solution)/shard_map/ppermute | solution.py:341
  35.1 1.0 %collective-permute-start.12 = (bf16[512,128]{1,0:T(8,128)(2,1)S(1)}, bf16[512,128]{1,0:T(8,128)(2,1)S(1)}, u32[]{:S(2)}, u32[]{:S(2)}) collective-permute-start(bf16[512,128]{1,0:T(8,128)(2,1)S(1)} %get-tuple-element.59), channel_id=1, source_target_pairs={{0,8},{4,12},{8,0},{12,4},{1,9},{5,13},{9,1},{13,5},{2,10},{6,14},... | collective-permute-start | bytes 393224 | tf_op jit(solution)/shard_map/ppermute | solution.py:341
  36.1 0.0 collective-permute-done.10.a_12_.a_8_
  36.1 1.3 %collective-permute-start.13 = (bf16[512,128]{1,0:T(8,128)(2,1)S(1)}, bf16[512,128]{1,0:T(8,128)(2,1)S(1)}, u32[]{:S(2)}, u32[]{:S(2)}) collective-permute-start(bf16[512,128]{1,0:T(8,128)(2,1)S(1)} %get-tuple-element.60), channel_id=1, source_target_pairs={{0,12},{4,8},{8,4},{12,0},{1,13},{5,9},{9,5},{13,1},{2,14},{6,10},... | collective-permute-start | bytes 393224 | tf_op jit(solution)/shard_map/ppermute | solution.py:341
  37.4 0.0 collective-permute-done.9.a_11_.a_7_
  37.4 0.0 collective-permute-done.8.a_10_.a_6_
  37.4 11.2 %shard_map.87 = (bf16[2,512,512]{2,1,0:T(8,128)(2,1)}, bf16[2,512,512]{2,1,0:T(8,128)(2,1)}, bf16[2,512,512]{2,1,0:T(8,128)(2,1)S(1)}, bf16[512,128]{1,0:T(8,128...) custom-call(s32[4]{0:T(128)S(1)} %pad_add_fusion.a_0_.info, ...), custom_call_target="tpu_custom_call" | custom-call | flops 25769803776 | bytes 1048576 | tf_op jit(solution)/shard_map/pallas_call | solution.py:373
  48.6 0.0 collective-permute-done.11.a_2_
  48.6 0.0 collective-permute-done.12.a_3_
  48.6 0.0 collective-permute-done.13.a_4_
  48.7 0.1 collective-permute-start.17
  48.7 1.4 %shard_map.89 = bf16[128,512]{1,0:T(8,128)(2,1)} custom-call(s32[4]{0:T(128)S(1)} %pad_add_fusion.a_0_.info, bf16[512,128]{1,0:T(8,128)(2,1)S(1)} %get-tuple-element.74.a_1_, bf16[512,128]{1,0:T(8,128)(2,1)S(1)} %collective-permute-done.11.a_2_, bf16[512,128]{1,0:T(8,128)(2,1)S(1)} %collective-permute-done.12.a_3_, ...), custom_call_target="tpu_custom_call" | custom-call | tf_op jit(solution)/shard_map/pallas_call | solution.py:368
  50.2 4.8 %all-to-all-start.1 = ((bf16[4,32,512]{2,1,0:T(8,128)(2,1)}), bf16[4,32,512]{2,1,0:T(8,128)(2,1)S(1)}, u32[]{:S(2)}, u32[]{:S(2)}) async-start(bf16[4,32,512]{2,1,0:T(8,128)(2,1)} %bitcast.3), calls=%async_computation.1 | async-start | bytes 262144 | tf_op jit(solution)/shard_map/all_to_all | solution.py:364
  55.0 1.6 %collective-permute-start.14 = (bf16[512,128]{1,0:T(8,128)(2,1)S(1)}, bf16[512,128]{1,0:T(8,128)(2,1)S(1)}, u32[]{:S(2)}, u32[]{:S(2)}) collective-permute-start(bf16[512,128]{1,0:T(8,128)(2,1)S(1)} %get-tuple-element.62), channel_id=1, source_target_pairs={{0,4},{4,0},{8,12},{12,8},{1,5},{5,1},{9,13},{13,9},{2,6},{6,2},{1... | collective-permute-start | bytes 393224 | tf_op jit(solution)/shard_map/ppermute | solution.py:341
  56.6 0.9 %collective-permute-start.15 = (bf16[512,128]{1,0:T(8,128)(2,1)S(1)}, bf16[512,128]{1,0:T(8,128)(2,1)S(1)}, u32[]{:S(2)}, u32[]{:S(2)}) collective-permute-start(bf16[512,128]{1,0:T(8,128)(2,1)S(1)} %get-tuple-element.63), channel_id=1, source_target_pairs={{0,8},{4,12},{8,0},{12,4},{1,9},{5,13},{9,1},{13,5},{2,10},{6,14},... | collective-permute-start | bytes 393224 | tf_op jit(solution)/shard_map/ppermute | solution.py:341
  57.5 1.0 %collective-permute-start.16 = (bf16[512,128]{1,0:T(8,128)(2,1)S(1)}, bf16[512,128]{1,0:T(8,128)(2,1)S(1)}, u32[]{:S(2)}, u32[]{:S(2)}) collective-permute-start(bf16[512,128]{1,0:T(8,128)(2,1)S(1)} %get-tuple-element.64), channel_id=1, source_target_pairs={{0,12},{4,8},{8,4},{12,0},{1,13},{5,9},{9,5},{13,1},{2,14},{6,10},... | collective-permute-start | bytes 393224 | tf_op jit(solution)/shard_map/ppermute | solution.py:341
  58.5 0.0 collective-permute-done.17.back
  58.5 1.7 %shard_map.88 = (bf16[2,512,512]{2,1,0:T(8,128)(2,1)}, bf16[2,512,512]{2,1,0:T(8,128)(2,1)}) custom-call(s32[4]{0:T(128)S(1)} %pad_add_fusion.a_0_.info, bf16[2,512,512]{2,1,0:T(8,128)(2,1)S(1)} %collective-permute-done.17.back, bf16[2,512,512]{2,1,0:T(8,128)(2,1)} %get-tuple-element.66.dk_in, ...), custom_call_target="tpu_custom_call", output_to_operand_aliasing={{0}: (2, {}), {1}: (3, {})} | custom-call | bytes 1048576 | tf_op jit(solution)/shard_map/pallas_call | solution.py:373
  60.1 0.7 %collective-permute-done.14.a_1_ = bf16[512,128]{1,0:T(8,128)(2,1)S(1)} collective-permute-done((bf16[512,128]{1,0:T(8,128)(2,1)S(1)}, bf16[512,128]{1,0:T(8,128)(2,1)S(1)}, u32[]{:S(2)}, u32[]{:S(2)}) %collective-permute-start.14) | collective-permute-done | bytes 131104 | tf_op jit(solution)/shard_map/ppermute | solution.py:341
  60.8 3.9 %collective-permute-done.15.a_2_ = bf16[512,128]{1,0:T(8,128)(2,1)S(1)} collective-permute-done((bf16[512,128]{1,0:T(8,128)(2,1)S(1)}, bf16[512,128]{1,0:T(8,128)(2,1)S(1)}, u32[]{:S(2)}, u32[]{:S(2)}) %collective-permute-start.15) | collective-permute-done | bytes 131104 | tf_op jit(solution)/shard_map/ppermute | solution.py:341
  64.7 0.0 collective-permute-done.16.a_3_
  64.7 0.0 all-to-all-done.1.a_4_
  64.7 0.8 %shard_map.90 = (bf16[128,512]{1,0:T(8,128)(2,1)}, bf16[32,2048]{1,0:T(8,128)(2,1)}) custom-call(bf16[512,128]{1,0:T(8,128)(2,1)S(1)} %get-tuple-element.70.a_0_, bf16[512,128]{1,0:T(8,128)(2,1)S(1)} %collective-permute-done.14.a_1_, bf16[512,128]{1,0:T(8,128)(2,1)S(1)} %collective-permute-done.15.a_2_, bf16[512,128]{1,0:T(8,128)(2,1)S(1)} %collective-permute-done.16.a_3_, ...), custom_call_target="tpu_custom_call" | custom-call | tf_op jit(solution)/shard_map/pallas_call | solution.py:368
Async XLA Ops:
  0.6 19.8 %collective-permute-start.6 = (bf16[2,512,512]{2,1,0:T(8,128)(2,1)}, bf16[2,512,512]{2,1,0:T(8,128)(2,1)S(1)}, u32[]{:S(2)}, u32[]{:S(2)}) collective-permute-start(bf16[2,512,512]{2,1,0:T(8,128)(2,1)} %a_5_.1), channel_id=1, source_target_pairs={{0,16},{16,0},{1,17},{17,1},{2,18},{18,2},{3,19},{19,3},{4,20},{20... | collective-permute-start | bytes 3145736 | tf_op jit(solution)/shard_map/ppermute | solution.py:341
  1.1 19.3 %collective-permute-start.7 = (bf16[2,512,512]{2,1,0:T(8,128)(2,1)}, bf16[2,512,512]{2,1,0:T(8,128)(2,1)S(1)}, u32[]{:S(2)}, u32[]{:S(2)}) collective-permute-start(bf16[2,512,512]{2,1,0:T(8,128)(2,1)} %a_6_.1), channel_id=1, source_target_pairs={{0,16},{16,0},{1,17},{17,1},{2,18},{18,2},{3,19},{19,3},{4,20},{20... | collective-permute-start | bytes 3145736 | tf_op jit(solution)/shard_map/ppermute | solution.py:341
  2.7 13.0 %all-to-all-start = ((bf16[4,32,512]{2,1,0:T(8,128)(2,1)}), bf16[4,32,512]{2,1,0:T(8,128)(2,1)S(1)}, u32[]{:S(2)}, u32[]{:S(2)}) async-start(bf16[4,32,512]{2,1,0:T(8,128)(2,1)} %shard_map.84), calls=%async_computation | async-start | bytes 262144 | tf_op jit(solution)/shard_map/all_to_all | solution.py:364
  9.0 6.7 %collective-permute-start.2 = (bf16[128,512]{1,0:T(8,128)(2,1)}, bf16[128,512]{1,0:T(8,128)(2,1)S(1)}, u32[]{:S(2)}, u32[]{:S(2)}) collective-permute-start(bf16[128,512]{1,0:T(8,128)(2,1)} %a_1_.3), channel_id=1, source_target_pairs={{0,12},{4,8},{8,4},{12,0},{1,13},{5,9},{9,5},{13,1},{2,14},{6,10},... | collective-permute-start | bytes 393224 | tf_op jit(solution)/shard_map/ppermute | solution.py:341
  11.5 7.5 %collective-permute-start.1 = (bf16[128,512]{1,0:T(8,128)(2,1)}, bf16[128,512]{1,0:T(8,128)(2,1)S(1)}, u32[]{:S(2)}, u32[]{:S(2)}) collective-permute-start(bf16[128,512]{1,0:T(8,128)(2,1)} %a_1_.3), channel_id=1, source_target_pairs={{0,8},{4,12},{8,0},{12,4},{1,9},{5,13},{9,1},{13,5},{2,10},{6,14},... | collective-permute-start | bytes 393224 | tf_op jit(solution)/shard_map/ppermute | solution.py:341
  12.0 8.0 %collective-permute-start = (bf16[128,512]{1,0:T(8,128)(2,1)}, bf16[128,512]{1,0:T(8,128)(2,1)S(1)}, u32[]{:S(2)}, u32[]{:S(2)}) collective-permute-start(bf16[128,512]{1,0:T(8,128)(2,1)} %a_1_.3), channel_id=1, source_target_pairs={{0,4},{4,0},{8,12},{12,8},{1,5},{5,1},{9,13},{13,9},{2,6},{6,2},{1... | collective-permute-start | bytes 393224 | tf_op jit(solution)/shard_map/ppermute | solution.py:341
  15.7 13.3 %collective-permute-start.5 = (bf16[128,512]{1,0:T(8,128)(2,1)S(1)}, bf16[128,512]{1,0:T(8,128)(2,1)S(1)}, u32[]{:S(2)}, u32[]{:S(2)}) collective-permute-start(bf16[128,512]{1,0:T(8,128)(2,1)S(1)} %bitcast.4), channel_id=1, source_target_pairs={{0,12},{4,8},{8,4},{12,0},{1,13},{5,9},{9,5},{13,1},{2,14},{6,10},... | collective-permute-start | bytes 393224 | tf_op jit(solution)/shard_map/ppermute | solution.py:341
  19.0 10.1 %collective-permute-start.4 = (bf16[128,512]{1,0:T(8,128)(2,1)S(1)}, bf16[128,512]{1,0:T(8,128)(2,1)S(1)}, u32[]{:S(2)}, u32[]{:S(2)}) collective-permute-start(bf16[128,512]{1,0:T(8,128)(2,1)S(1)} %bitcast.5), channel_id=1, source_target_pairs={{0,8},{4,12},{8,0},{12,4},{1,9},{5,13},{9,1},{13,5},{2,10},{6,14},... | collective-permute-start | bytes 393224 | tf_op jit(solution)/shard_map/ppermute | solution.py:341
  20.0 9.1 %collective-permute-start.3 = (bf16[128,512]{1,0:T(8,128)(2,1)S(1)}, bf16[128,512]{1,0:T(8,128)(2,1)S(1)}, u32[]{:S(2)}, u32[]{:S(2)}) collective-permute-start(bf16[128,512]{1,0:T(8,128)(2,1)S(1)} %bitcast.6), channel_id=1, source_target_pairs={{0,4},{4,0},{8,12},{12,8},{1,5},{5,1},{9,13},{13,9},{2,6},{6,2},{1... | collective-permute-start | bytes 393224 | tf_op jit(solution)/shard_map/ppermute | solution.py:341
  30.0 6.1 %collective-permute-start.10 = (f32[4,4,512]{2,1,0:T(4,128)S(1)}, f32[4,4,512]{2,1,0:T(4,128)S(1)}, u32[]{:S(2)}, u32[]{:S(2)}) collective-permute-start(f32[4,4,512]{2,1,0:T(4,128)S(1)} %get-tuple-element.45.a_9_.a_5_), channel_id=1, source_target_pairs={{0,12},{4,8},{8,4},{12,0},{1,13},{5,9},{9,5},{13,1},{2,14},{6,10},... | collective-permute-start | bytes 98312 | tf_op jit(solution)/shard_map/ppermute | solution.py:341
  32.1 5.3 %collective-permute-start.9 = (f32[4,4,512]{2,1,0:T(4,128)S(1)}, f32[4,4,512]{2,1,0:T(4,128)S(1)}, u32[]{:S(2)}, u32[]{:S(2)}) collective-permute-start(f32[4,4,512]{2,1,0:T(4,128)S(1)} %get-tuple-element.45.a_9_.a_5_), channel_id=1, source_target_pairs={{0,8},{4,12},{8,0},{12,4},{1,9},{5,13},{9,1},{13,5},{2,10},{6,14},... | collective-permute-start | bytes 98312 | tf_op jit(solution)/shard_map/ppermute | solution.py:341
  33.1 4.3 %collective-permute-start.8 = (f32[4,4,512]{2,1,0:T(4,128)S(1)}, f32[4,4,512]{2,1,0:T(4,128)S(1)}, u32[]{:S(2)}, u32[]{:S(2)}) collective-permute-start(f32[4,4,512]{2,1,0:T(4,128)S(1)} %get-tuple-element.45.a_9_.a_5_), channel_id=1, source_target_pairs={{0,4},{4,0},{8,12},{12,8},{1,5},{5,1},{9,13},{13,9},{2,6},{6,2},{1... | collective-permute-start | bytes 98312 | tf_op jit(solution)/shard_map/ppermute | solution.py:341
  33.6 15.1 %collective-permute-start.11 = (bf16[512,128]{1,0:T(8,128)(2,1)S(1)}, bf16[512,128]{1,0:T(8,128)(2,1)S(1)}, u32[]{:S(2)}, u32[]{:S(2)}) collective-permute-start(bf16[512,128]{1,0:T(8,128)(2,1)S(1)} %get-tuple-element.58), channel_id=1, source_target_pairs={{0,4},{4,0},{8,12},{12,8},{1,5},{5,1},{9,13},{13,9},{2,6},{6,2},{1... | collective-permute-start | bytes 393224 | tf_op jit(solution)/shard_map/ppermute | solution.py:341
  35.1 13.5 %collective-permute-start.12 = (bf16[512,128]{1,0:T(8,128)(2,1)S(1)}, bf16[512,128]{1,0:T(8,128)(2,1)S(1)}, u32[]{:S(2)}, u32[]{:S(2)}) collective-permute-start(bf16[512,128]{1,0:T(8,128)(2,1)S(1)} %get-tuple-element.59), channel_id=1, source_target_pairs={{0,8},{4,12},{8,0},{12,4},{1,9},{5,13},{9,1},{13,5},{2,10},{6,14},... | collective-permute-start | bytes 393224 | tf_op jit(solution)/shard_map/ppermute | solution.py:341
  36.1 12.5 %collective-permute-start.13 = (bf16[512,128]{1,0:T(8,128)(2,1)S(1)}, bf16[512,128]{1,0:T(8,128)(2,1)S(1)}, u32[]{:S(2)}, u32[]{:S(2)}) collective-permute-start(bf16[512,128]{1,0:T(8,128)(2,1)S(1)} %get-tuple-element.60), channel_id=1, source_target_pairs={{0,12},{4,8},{8,4},{12,0},{1,13},{5,9},{9,5},{13,1},{2,14},{6,10},... | collective-permute-start | bytes 393224 | tf_op jit(solution)/shard_map/ppermute | solution.py:341
  48.7 9.8 %collective-permute-start.17 = (bf16[2,512,512]{2,1,0:T(8,128)(2,1)S(1)}, bf16[2,512,512]{2,1,0:T(8,128)(2,1)S(1)}, u32[]{:S(2)}, u32[]{:S(2)}) collective-permute-start(bf16[2,512,512]{2,1,0:T(8,128)(2,1)S(1)} %get-tuple-element.65), channel_id=1, source_target_pairs={{0,16},{16,0},{1,17},{17,1},{2,18},{18,2},{3,19},{19,3},{4,20},{20... | collective-permute-start | bytes 3145736 | tf_op jit(solution)/shard_map/ppermute | solution.py:341
  50.2 14.6 %all-to-all-start.1 = ((bf16[4,32,512]{2,1,0:T(8,128)(2,1)}), bf16[4,32,512]{2,1,0:T(8,128)(2,1)S(1)}, u32[]{:S(2)}, u32[]{:S(2)}) async-start(bf16[4,32,512]{2,1,0:T(8,128)(2,1)} %bitcast.3), calls=%async_computation.1 | async-start | bytes 262144 | tf_op jit(solution)/shard_map/all_to_all | solution.py:364
  55.0 5.9 %collective-permute-start.14 = (bf16[512,128]{1,0:T(8,128)(2,1)S(1)}, bf16[512,128]{1,0:T(8,128)(2,1)S(1)}, u32[]{:S(2)}, u32[]{:S(2)}) collective-permute-start(bf16[512,128]{1,0:T(8,128)(2,1)S(1)} %get-tuple-element.62), channel_id=1, source_target_pairs={{0,4},{4,0},{8,12},{12,8},{1,5},{5,1},{9,13},{13,9},{2,6},{6,2},{1... | collective-permute-start | bytes 393224 | tf_op jit(solution)/shard_map/ppermute | solution.py:341
  56.6 8.1 %collective-permute-start.15 = (bf16[512,128]{1,0:T(8,128)(2,1)S(1)}, bf16[512,128]{1,0:T(8,128)(2,1)S(1)}, u32[]{:S(2)}, u32[]{:S(2)}) collective-permute-start(bf16[512,128]{1,0:T(8,128)(2,1)S(1)} %get-tuple-element.63), channel_id=1, source_target_pairs={{0,8},{4,12},{8,0},{12,4},{1,9},{5,13},{9,1},{13,5},{2,10},{6,14},... | collective-permute-start | bytes 393224 | tf_op jit(solution)/shard_map/ppermute | solution.py:341
  57.5 7.3 %collective-permute-start.16 = (bf16[512,128]{1,0:T(8,128)(2,1)S(1)}, bf16[512,128]{1,0:T(8,128)(2,1)S(1)}, u32[]{:S(2)}, u32[]{:S(2)}) collective-permute-start(bf16[512,128]{1,0:T(8,128)(2,1)S(1)} %get-tuple-element.64), channel_id=1, source_target_pairs={{0,12},{4,8},{8,4},{12,0},{1,13},{5,9},{9,5},{13,1},{2,14},{6,10},... | collective-permute-start | bytes 393224 | tf_op jit(solution)/shard_map/ppermute | solution.py:341

commit v4 on v3

--- a/solution.py
+++ b/solution.py
@@ -29,6 +29,14 @@
 
 def lane_scale():
     return jnp.full((1, PAIR), 1.0 / math.sqrt(HEAD_DIM), F32).astype(BF16)
+
+
+def pair_lanes(pair):
+    return pl.ds(pl.multiple_of(pair * PAIR, PAIR), PAIR)
+
+
+def head_features(pair, u):
+    return pl.ds(pl.multiple_of(pair * PAIR + u * HEAD_DIM, HEAD_DIM), HEAD_DIM)
 
 
 def stack_slots(refs, slots, lanes):
@@ -90,19 +98,21 @@
 
 
 def forward_kernel(n, rows, info, *refs):
-    q = refs[:n]
-    k_own, v_own, k_oth, v_oth, lse_ref, top_ref, out_ref, exp_ref, kt_ref, v_ref = refs[n:]
-    first_pair = pl.program_id(0) * lse_ref.shape[0]
+    q = [refs[0], refs[n - 1], *refs[1 : n - 1]]
+    k_own, v_own, k_oth, v_oth, lse_ref, top_ref, out_ref, exp_ref, kt_ref, v_ref, q_ref = refs[n:]
+    step = k_own.shape[2] // PAIR
+    first_pair = pl.program_id(0) * step
 
     def run(blocks, rest):
-        def sources(own, oth, lanes):
-            return chunked([own[0, :, lanes], oth[0, :, lanes]])
+        def sources(own, oth, p):
+            return chunked([own[0, :, p * PAIR : (p + 1) * PAIR], oth[info[0], :, pair_lanes(first_pair + p)]])
 
         ks, vts, qts = {}, {}, {}
-        for p in range(lse_ref.shape[0]):
-            lanes = slice(p * PAIR, (p + 1) * PAIR)
-            ks[p] = sources(k_own, k_oth, lanes)
-            vs = sources(v_own, v_oth, lanes)
+        for p in range(step):
+            lanes = pair_lanes(first_pair + p)
+            q_ref[:, lanes] = q[0][:, p * PAIR : (p + 1) * PAIR]
+            ks[p] = sources(k_own, k_oth, p)
+            vs = sources(v_own, v_oth, p)
             vt = [x.T for x in vs]
             for c in range(len(vs)):
                 kt_ref[first_pair + p, c] = ks[p][c].T
@@ -112,7 +122,7 @@
             for u in range(2):
                 vts[p, u] = [jnp.concatenate([x[u * HEAD_DIM : (u + 1) * HEAD_DIM], ones], axis=0) for x in vt]
             for b, slots in enumerate(blocks):
-                qts[p, b] = (stack_slots(q, slots, lanes) * lane_scale()).T
+                qts[p, b] = (stack_slots([q_ref, *q[1:]], slots, lanes) * lane_scale()).T
 
         def scores(chain):
             p, b, u = chain
@@ -134,11 +144,11 @@
                 o = part if o is None else o + part
             total = o[HEAD_DIM : HEAD_DIM + 1]
             cols = pl.ds(blocks[b][0] * rows, rows * len(blocks[b]))
-            lse_ref[p, u : u + 1, cols] = top + jnp.log(total)
-            top_ref[p, u : u + 1, cols] = top
-            out_ref[p * PAIR + u * HEAD_DIM : p * PAIR + (u + 1) * HEAD_DIM, cols] = o[:HEAD_DIM] / total
-
-        chains = [(p, b, u) for p in range(lse_ref.shape[0]) for b in range(len(blocks)) for u in range(2)]
+            lse_ref[first_pair + p, u : u + 1, cols] = top + jnp.log(total)
+            top_ref[first_pair + p, u : u + 1, cols] = top
+            out_ref[head_features(first_pair + p, u), cols] = o[:HEAD_DIM] / total
+
+        chains = [(p, b, u) for p in range(step) for b in range(len(blocks)) for u in range(2)]
         ahead = scores(chains[0])
         for i, chain in enumerate(chains):
             now = ahead
@@ -148,9 +158,10 @@
         for slots in rest:
             width = rows * len(slots)
             cols = pl.ds(slots[0] * rows, width)
-            lse_ref[:, :, cols] = jnp.zeros((lse_ref.shape[0], 2, width), F32)
-            top_ref[:, :, cols] = jnp.zeros((lse_ref.shape[0], 2, width), F32)
-            out_ref[:, cols] = jnp.zeros((out_ref.shape[0], width), F32)
+            for p in range(step):
+                lse_ref[first_pair + p, :, cols] = jnp.zeros((2, width), F32)
+                top_ref[first_pair + p, :, cols] = jnp.zeros((2, width), F32)
+                out_ref[pair_lanes(first_pair + p), cols] = jnp.zeros((PAIR, width), F32)
 
     for_valid_blocks(n, rows, info, run)
 
@@ -193,20 +204,20 @@
     top_ref, exp_ref, kt_ref, v_ref = refs[3 * n : 3 * n + 4]
     dk_own, dv_own, d_oth = refs[3 * n + 4 : 3 * n + 7]
     dq = refs[3 * n + 7 :]
-    first_pair = pl.program_id(0) * top_ref.shape[0]
+    pairs = dk_own.shape[2] // PAIR
+    first_pair = pl.program_id(0) * pairs
     scale = 1.0 / math.sqrt(HEAD_DIM)
 
     def ordered(j, p, kind, u, slots):
-        line = stats[j][p, 2 * kind + u : 2 * kind + u + 1]
+        line = stats[j][first_pair + p, 2 * kind + u : 2 * kind + u + 1]
         if rows % 128:
             return line[:, slots[0] * rows : (slots[-1] + 1) * rows]
         return jnp.concatenate([line[:, (k ^ j) * rows : ((k ^ j) + 1) * rows] for k in slots], axis=1)
 
     def run(blocks, rest):
         vs, kt, operands = {}, {}, {}
-        pairs = stats[0].shape[0]
         for p in range(pairs):
-            lanes = slice(p * PAIR, (p + 1) * PAIR)
+            lanes = pair_lanes(first_pair + p)
             chunks = range(v_ref.shape[1])
             vs[p] = [with_ones(v_ref[first_pair + p, c]) for c in chunks]
             kt[p] = [kt_ref[first_pair + p, c] for c in chunks]
@@ -220,7 +231,7 @@
                         [ordered(j, p, 0, u, slots) for j in range(n)], [ordered(j, p, 1, u, slots) for j in range(n)]
                     )
                     operands[p, b, u] = (
-                        jnp.exp(top_ref[p, u : u + 1, cols] - lse),
+                        jnp.exp(top_ref[first_pair + p, u : u + 1, cols] - lse),
                         jnp.concatenate([head_rows(gt, u), minus_rows(delta)], axis=0),
                         qb * lane_mask(u, 1.0),
                         gb * lane_mask(u, 1.0),
@@ -253,8 +264,8 @@
                 at = slice(c * size, (c + 1) * size)
                 dk_own[0, at, lanes] = dks[p, c].astype(BF16)
                 dv_own[0, at, lanes] = dvs[p, c].astype(BF16)
-                d_oth[0, at, lanes] = dks[p, half + c].astype(BF16)
-                d_oth[1, at, lanes] = dvs[p, half + c].astype(BF16)
+                d_oth[0, at, pair_lanes(first_pair + p)] = dks[p, half + c].astype(BF16)
+                d_oth[1, at, pair_lanes(first_pair + p)] = dvs[p, half + c].astype(BF16)
 
         chains = [(p, b, u) for p in range(pairs) for b in range(len(blocks)) for u in range(2)]
         items = [(chain, c) for chain in chains for c in range(count)]
@@ -268,14 +279,14 @@
             if c == count - 1:
                 p, b, u = chain
                 total = dqs[chain] * scale
-                feat = slice(p * PAIR + u * HEAD_DIM, p * PAIR + (u + 1) * HEAD_DIM)
                 for j, k in enumerate(blocks[b]):
-                    dq[k][feat] = total[:, j * rows : (j + 1) * rows].astype(BF16)
+                    dq[k][head_features(first_pair + p, u)] = total[:, j * rows : (j + 1) * rows].astype(BF16)
                 if i + 1 == len(items) or items[i + 1][0][0] != p:
                     store(p)
         for slots in rest:
             for k in slots:
-                dq[k][...] = jnp.zeros_like(dq[k])
+                for p in range(pairs):
+                    dq[k][pair_lanes(first_pair + p)] = jnp.zeros((PAIR, rows), BF16)
 
     for_valid_blocks(n, rows, info, run)
 
@@ -382,14 +393,10 @@
         )(info, *args)
 
     lanes = step * PAIR
-    slot_in = [pl.BlockSpec((rows, lanes), lambda h, info: (0, h))] * n
-    slot_t = [pl.BlockSpec((lanes, rows), lambda h, info: (h, 0))] * n
+    slot_in = pl.BlockSpec((rows, lanes), lambda h, info: (0, h))
     own = pl.BlockSpec((1, src, lanes), lambda h, info: (info[0], 0, h))
     away = pl.BlockSpec((1, src, lanes), lambda h, info: (1 - info[0], 0, h))
     oth = pl.BlockSpec((2, src, lanes), lambda h, info: (0, 0, h))
-    lse_spec = pl.BlockSpec((step, 2, tgt), lambda h, info: (h, 0, 0))
-    out_spec = pl.BlockSpec((lanes, tgt), lambda h, info: (h, 0))
-    stats_spec = pl.BlockSpec((step, 4, tgt), lambda h, info: (h, 0, 0))
 
     q = gather(queries)
     k_oth, v_oth = xor_permute(keys, "grp", 2, 1), xor_permute(values, "grp", 2, 1)
@@ -406,14 +413,14 @@
     chunk, per = min(256, src), rows * len(target_blocks(n, rows)[0])
     exps = (pairs, 2 * (tgt // per), 2 * src // chunk, chunk, per)
     count = 2 * src // chunk
-    lse, top, out_t, exps, kt, v = call(
+    lse, top, out_t, exps, kt, v, q_own = call(
         lambda *a: forward_kernel(n, rows, *a),
-        slot_in + [own] * 4,
-        [lse_spec, lse_spec, out_spec, whole, whole, whole],
+        [slot_in] + [whole] * (n - 1) + [own, own, whole, whole],
+        [whole] * 7,
         [sds((pairs, 2, tgt), F32)] * 2
         + [sds((width, tgt), F32), sds(exps, BF16)]
-        + [sds((pairs, count, PAIR, chunk), BF16), sds((pairs, count, chunk, PAIR), BF16)],
-        [stay(queries), *q[1:], stay(keys), stay(values), k_oth, v_oth],
+        + [sds((pairs, count, PAIR, chunk), BF16), sds((pairs, count, chunk, PAIR), BF16), sds((rows, width), BF16)],
+        [stay(queries), *q[2:], q[1], stay(keys), stay(values), k_oth, v_oth],
         flops=2 * flop,
     )
     stats, *sends = plain(
@@ -432,10 +439,10 @@
     outs = [sends[0]] + [xor_permute(sends[k], "seq", n, k) for k in range(1, n)]
     grads = call(
         lambda *a: backward_kernel(n, rows, *a),
-        slot_in + slot_in + [stats_spec] * n + [lse_spec, whole, whole, whole],
-        [own, own, oth] + slot_t,
+        [whole] * (3 * n + 4),
+        [own, own] + [whole] * (n + 1),
         [sds((2, src, width), BF16)] * 3 + [sds((width, rows), BF16)] * n,
-        [stay(queries), *q[1:], *g, *all_stats, top, exps, kt, v],
+        [q_own, *q[1:], *g, *all_stats, top, exps, kt, v],
         flops=4 * flop,
     )
     (dk, dv, d_oth, *dq), outs = lax.optimization_barrier((grads, outs))

time: 66 us -> 65.2 us (0.988)
  Pallas kernels: 26.1 us -> 25.3 us
    pallas_call x3, Pallas kernels: 21.4 us -> 20.7 us  [call(): pl.pallas_call(kernel, grid_spec=pltpu.PrefetchScalarGridSpec(num_scalar_...]
  transfers between devices with their start and end apart: 20 -> 20, of which waited for: 3 -> 3; matrix products, arithmetic and copies ran while one was open for 1% -> 1% of each run, Pallas kernels for 37% -> 36%
where the time goes in v4:
time: 65.2 us; the launch traced here: 64.7 us
  starting transfers between devices  30.9 us (47%)
  Pallas kernels  25.3 us (39%)
  waiting for transfers between devices  7.11 us (11%)
  other arithmetic  0.73 us (1%)
  between operations  0.71 us (1%)
    pallas_call x3, Pallas kernels, call(): pl.pallas_call(kernel, grid_spec=pltpu.PrefetchScalarGridSpec(num_scalar_...  20.7 us
    ppermute x18, starting transfers between devices, xor_permute(): return lax.ppermute(x, axis, [(i, i ^ k) for i in range(size)])  19.8 us
    all_to_all x2, starting transfers between devices, exchange(): return lax.all_to_all(x, 'head', split_axis=0, concat_axis=0, tiled=True)  11.1 us
    ppermute x18, waiting for transfers between devices, xor_permute(): return lax.ppermute(x, axis, [(i, i ^ k) for i in range(size)])  7.1 us
    pallas_call x3, Pallas kernels, plain(): pl.pallas_call(kernel, in_specs=in_specs, out_specs=out_specs, out_shape=...  3.13 us
    pallas_call x1, Pallas kernels, local(): pl.pallas_call(split_kernel, in_specs=[pl.BlockSpec(memory_space=pltpu.HB...  1.49 us
  transfers between devices with their start and end apart: 20, of which 3 were waited for; matrix products, arithmetic and copies ran while one was open for 1% of the time, Pallas kernels for 36%

profile of v4, /device:TPU:0, one launch (start us, length us, event | category | flops | bytes accessed | tf_op | source)
XLA Modules:
  0.0 64.7 jit_solution(10497624974020878278)
XLA Ops:
  0.6 0.5 collective-permute-start.3
  1.1 0.1 collective-permute-start.4
  1.2 1.5 %shard_map.85 = bf16[4,32,512]{2,1,0:T(8,128)(2,1)} custom-call(bf16[32,2048]{1,0:T(8,128)(2,1)} %grad.1), custom_call_target="tpu_custom_call" | custom-call | tf_op jit(solution)/shard_map/pallas_call | solution.py:403
  2.7 6.3 %all-to-all-start = ((bf16[4,32,512]{2,1,0:T(8,128)(2,1)}), bf16[4,32,512]{2,1,0:T(8,128)(2,1)S(1)}, u32[]{:S(2)}, u32[]{:S(2)}) async-start(bf16[4,32,512]{2,1,0:T(8,128)(2,1)} %shard_map.85), calls=%async_computation | async-start | bytes 262144 | tf_op jit(solution)/shard_map/all_to_all | solution.py:375
  9.0 2.4 %collective-permute-start.1 = (bf16[128,512]{1,0:T(8,128)(2,1)}, bf16[128,512]{1,0:T(8,128)(2,1)S(1)}, u32[]{:S(2)}, u32[]{:S(2)}) collective-permute-start(bf16[128,512]{1,0:T(8,128)(2,1)} %a_1_.1), channel_id=1, source_target_pairs={{0,12},{4,8},{8,4},{12,0},{1,13},{5,9},{9,5},{13,1},{2,14},{6,10},... | collective-permute-start | bytes 393224 | tf_op jit(solution)/shard_map/ppermute | solution.py:352
  11.5 0.5 collective-permute-start
  12.0 0.5 collective-permute-start.2
  12.5 0.7 %pad_add_fusion.a_0_.info = s32[4]{0:T(128)S(1)} fusion(s32[2]{0:T(128)} %param.9, s32[1]{0:T(128)} %bitcast.1, s32[1]{0:T(128)} %bitcast), kind=kLoop, calls=%fused_computation | loop fusion | flops 8 | bytes 32 | tf_op jit(solution)/shard_map/concatenate | solution.py:369
  13.3 2.5 %collective-permute-done.1.a_3_.a_4_ = bf16[128,512]{1,0:T(8,128)(2,1)S(1)} collective-permute-done((bf16[128,512]{1,0:T(8,128)(2,1)}, bf16[128,512]{1,0:T(8,128)(2,1)S(1)}, u32[]{:S(2)}, u32[]{:S(2)}) %collective-permute-start.1) | collective-permute-done | bytes 131104 | tf_op jit(solution)/shard_map/ppermute | solution.py:352
  15.7 0.0 all-to-all-done
  15.7 3.3 %collective-permute-start.7 = (bf16[128,512]{1,0:T(8,128)(2,1)S(1)}, bf16[128,512]{1,0:T(8,128)(2,1)S(1)}, u32[]{:S(2)}, u32[]{:S(2)}) collective-permute-start(bf16[128,512]{1,0:T(8,128)(2,1)S(1)} %bitcast.4), channel_id=1, source_target_pairs={{0,12},{4,8},{8,4},{12,0},{1,13},{5,9},{9,5},{13,1},{2,14},{6,10},... | collective-permute-start | bytes 393224 | tf_op jit(solution)/shard_map/ppermute | solution.py:352
  19.0 0.0 collective-permute-done.a_2_.a_3_
  19.0 1.0 %collective-permute-start.6 = (bf16[128,512]{1,0:T(8,128)(2,1)S(1)}, bf16[128,512]{1,0:T(8,128)(2,1)S(1)}, u32[]{:S(2)}, u32[]{:S(2)}) collective-permute-start(bf16[128,512]{1,0:T(8,128)(2,1)S(1)} %bitcast.5), channel_id=1, source_target_pairs={{0,8},{4,12},{8,0},{12,4},{1,9},{5,13},{9,1},{13,5},{2,10},{6,14},... | collective-permute-start | bytes 393224 | tf_op jit(solution)/shard_map/ppermute | solution.py:352
  20.0 0.0 collective-permute-done.2.a_4_.a_2_
  20.0 0.5 collective-permute-start.5
  20.5 0.0 collective-permute-done.3.a_7_
  20.5 0.0 collective-permute-done.4.a_8_
  20.5 8.6 %shard_map.84 = (f32[4,2,512]{2,1,0:T(2,128)S(1)}, f32[4,2,512]{2,1,0:T(2,128)S(1)}, f32[512,512]{1,0:T(8,128)S(1)}, bf16[4,4,4,256,256]{4,3,2,1,0:T(8,128)(2,1)...) custom-call(s32[4]{0:T(128)S(1)} %pad_add_fusion.a_0_.info, ...), custom_call_target="tpu_custom_call" | custom-call | flops 12884901888 | bytes 1048576 | tf_op jit(solution)/shard_map/pallas_call | solution.py:384
  29.1 0.0 collective-permute-done.7.a_4_.a_8_
  29.1 0.0 collective-permute-done.6.a_3_.a_7_
  29.1 0.0 collective-permute-done.5.a_2_.a_6_
  29.1 0.9 %shard_map.86 = (f32[4,4,512]{2,1,0:T(4,128)S(1)}, bf16[512,128]{1,0:T(8,128)(2,1)S(1)}, bf16[512,128]{1,0:T(8,128)(2,1)S(1)}, bf16[512,128]{1,0:T(8,128)(2,1)S(1)}, bf16[512,128]{1,0:T(8,128)(2,1)S(1)}) custom-call(s32[4]{0:T(128)S(1)} %pad_add_fusion.a_0_.info, bf16[128,512]{1,0:T(8,128)(2,1)S(1)} %bitcast.7, ...), custom_call_target="tpu_custom_call" | custom-call | tf_op jit(solution)/shard_map/pallas_call | solution.py:379
  30.1 2.1 %collective-permute-start.10 = (f32[4,4,512]{2,1,0:T(4,128)S(1)}, f32[4,4,512]{2,1,0:T(4,128)S(1)}, u32[]{:S(2)}, u32[]{:S(2)}) collective-permute-start(f32[4,4,512]{2,1,0:T(4,128)S(1)} %get-tuple-element.47.a_9_.a_5_), channel_id=1, source_target_pairs={{0,12},{4,8},{8,4},{12,0},{1,13},{5,9},{9,5},{13,1},{2,14},{6,10},... | collective-permute-start | bytes 98312 | tf_op jit(solution)/shard_map/ppermute | solution.py:352
  32.1 1.0 %collective-permute-start.9 = (f32[4,4,512]{2,1,0:T(4,128)S(1)}, f32[4,4,512]{2,1,0:T(4,128)S(1)}, u32[]{:S(2)}, u32[]{:S(2)}) collective-permute-start(f32[4,4,512]{2,1,0:T(4,128)S(1)} %get-tuple-element.47.a_9_.a_5_), channel_id=1, source_target_pairs={{0,8},{4,12},{8,0},{12,4},{1,9},{5,13},{9,1},{13,5},{2,10},{6,14},... | collective-permute-start | bytes 98312 | tf_op jit(solution)/shard_map/ppermute | solution.py:352
  33.1 0.5 collective-permute-start.8
  33.6 1.6 %collective-permute-start.11 = (bf16[512,128]{1,0:T(8,128)(2,1)S(1)}, bf16[512,128]{1,0:T(8,128)(2,1)S(1)}, u32[]{:S(2)}, u32[]{:S(2)}) collective-permute-start(bf16[512,128]{1,0:T(8,128)(2,1)S(1)} %get-tuple-element.60), channel_id=1, source_target_pairs={{0,4},{4,0},{8,12},{12,8},{1,5},{5,1},{9,13},{13,9},{2,6},{6,2},{1... | collective-permute-start | bytes 393224 | tf_op jit(solution)/shard_map/ppermute | solution.py:352
  35.2 1.0 %collective-permute-start.12 = (bf16[512,128]{1,0:T(8,128)(2,1)S(1)}, bf16[512,128]{1,0:T(8,128)(2,1)S(1)}, u32[]{:S(2)}, u32[]{:S(2)}) collective-permute-start(bf16[512,128]{1,0:T(8,128)(2,1)S(1)} %get-tuple-element.61), channel_id=1, source_target_pairs={{0,8},{4,12},{8,0},{12,4},{1,9},{5,13},{9,1},{13,5},{2,10},{6,14},... | collective-permute-start | bytes 393224 | tf_op jit(solution)/shard_map/ppermute | solution.py:352
  36.2 0.0 collective-permute-done.10.a_12_.a_8_
  36.2 1.3 %collective-permute-start.13 = (bf16[512,128]{1,0:T(8,128)(2,1)S(1)}, bf16[512,128]{1,0:T(8,128)(2,1)S(1)}, u32[]{:S(2)}, u32[]{:S(2)}) collective-permute-start(bf16[512,128]{1,0:T(8,128)(2,1)S(1)} %get-tuple-element.62), channel_id=1, source_target_pairs={{0,12},{4,8},{8,4},{12,0},{1,13},{5,9},{9,5},{13,1},{2,14},{6,10},... | collective-permute-start | bytes 393224 | tf_op jit(solution)/shard_map/ppermute | solution.py:352
  37.5 0.0 collective-permute-done.9.a_11_.a_7_
  37.5 0.0 collective-permute-done.8.a_10_.a_6_
  37.5 10.4 %shard_map.87 = (bf16[2,512,512]{2,1,0:T(8,128)(2,1)}, bf16[2,512,512]{2,1,0:T(8,128)(2,1)}, bf16[2,512,512]{2,1,0:T(8,128)(2,1)S(1)}, bf16[512,128]{1,0:T(8,128...) custom-call(s32[4]{0:T(128)S(1)} %pad_add_fusion.a_0_.info, ...), custom_call_target="tpu_custom_call" | custom-call | flops 25769803776 | bytes 1048576 | tf_op jit(solution)/shard_map/pallas_call | solution.py:384
  47.9 0.0 collective-permute-done.11.a_2_
  47.9 0.0 collective-permute-done.12.a_3_
  47.9 0.0 collective-permute-done.13.a_4_
  47.9 0.1 collective-permute-start.17
  48.0 1.4 %shard_map.89 = bf16[128,512]{1,0:T(8,128)(2,1)} custom-call(s32[4]{0:T(128)S(1)} %pad_add_fusion.a_0_.info, bf16[512,128]{1,0:T(8,128)(2,1)S(1)} %get-tuple-element.76.a_1_, bf16[512,128]{1,0:T(8,128)(2,1)S(1)} %collective-permute-done.11.a_2_, bf16[512,128]{1,0:T(8,128)(2,1)S(1)} %collective-permute-done.12.a_3_, ...), custom_call_target="tpu_custom_call" | custom-call | tf_op jit(solution)/shard_map/pallas_call | solution.py:379
  49.4 4.8 %all-to-all-start.1 = ((bf16[4,32,512]{2,1,0:T(8,128)(2,1)}), bf16[4,32,512]{2,1,0:T(8,128)(2,1)S(1)}, u32[]{:S(2)}, u32[]{:S(2)}) async-start(bf16[4,32,512]{2,1,0:T(8,128)(2,1)} %bitcast.3), calls=%async_computation.1 | async-start | bytes 262144 | tf_op jit(solution)/shard_map/all_to_all | solution.py:375
  54.2 1.6 %collective-permute-start.14 = (bf16[512,128]{1,0:T(8,128)(2,1)S(1)}, bf16[512,128]{1,0:T(8,128)(2,1)S(1)}, u32[]{:S(2)}, u32[]{:S(2)}) collective-permute-start(bf16[512,128]{1,0:T(8,128)(2,1)S(1)} %get-tuple-element.64), channel_id=1, source_target_pairs={{0,4},{4,0},{8,12},{12,8},{1,5},{5,1},{9,13},{13,9},{2,6},{6,2},{1... | collective-permute-start | bytes 393224 | tf_op jit(solution)/shard_map/ppermute | solution.py:352
  55.8 0.9 %collective-permute-start.15 = (bf16[512,128]{1,0:T(8,128)(2,1)S(1)}, bf16[512,128]{1,0:T(8,128)(2,1)S(1)}, u32[]{:S(2)}, u32[]{:S(2)}) collective-permute-start(bf16[512,128]{1,0:T(8,128)(2,1)S(1)} %get-tuple-element.65), channel_id=1, source_target_pairs={{0,8},{4,12},{8,0},{12,4},{1,9},{5,13},{9,1},{13,5},{2,10},{6,14},... | collective-permute-start | bytes 393224 | tf_op jit(solution)/shard_map/ppermute | solution.py:352
  56.7 1.0 %collective-permute-start.16 = (bf16[512,128]{1,0:T(8,128)(2,1)S(1)}, bf16[512,128]{1,0:T(8,128)(2,1)S(1)}, u32[]{:S(2)}, u32[]{:S(2)}) collective-permute-start(bf16[512,128]{1,0:T(8,128)(2,1)S(1)} %get-tuple-element.66), channel_id=1, source_target_pairs={{0,12},{4,8},{8,4},{12,0},{1,13},{5,9},{9,5},{13,1},{2,14},{6,10},... | collective-permute-start | bytes 393224 | tf_op jit(solution)/shard_map/ppermute | solution.py:352
  57.7 0.0 collective-permute-done.17.back
  57.7 1.7 %shard_map.88 = (bf16[2,512,512]{2,1,0:T(8,128)(2,1)}, bf16[2,512,512]{2,1,0:T(8,128)(2,1)}) custom-call(s32[4]{0:T(128)S(1)} %pad_add_fusion.a_0_.info, bf16[2,512,512]{2,1,0:T(8,128)(2,1)S(1)} %collective-permute-done.17.back, bf16[2,512,512]{2,1,0:T(8,128)(2,1)} %get-tuple-element.68.dk_in, ...), custom_call_target="tpu_custom_call", output_to_operand_aliasing={{0}: (2, {}), {1}: (3, {})} | custom-call | bytes 1048576 | tf_op jit(solution)/shard_map/pallas_call | solution.py:384
  59.3 0.7 %collective-permute-done.14.a_1_ = bf16[512,128]{1,0:T(8,128)(2,1)S(1)} collective-permute-done((bf16[512,128]{1,0:T(8,128)(2,1)S(1)}, bf16[512,128]{1,0:T(8,128)(2,1)S(1)}, u32[]{:S(2)}, u32[]{:S(2)}) %collective-permute-start.14) | collective-permute-done | bytes 131104 | tf_op jit(solution)/shard_map/ppermute | solution.py:352
  60.0 3.9 %collective-permute-done.15.a_2_ = bf16[512,128]{1,0:T(8,128)(2,1)S(1)} collective-permute-done((bf16[512,128]{1,0:T(8,128)(2,1)S(1)}, bf16[512,128]{1,0:T(8,128)(2,1)S(1)}, u32[]{:S(2)}, u32[]{:S(2)}) %collective-permute-start.15) | collective-permute-done | bytes 131104 | tf_op jit(solution)/shard_map/ppermute | solution.py:352
  63.9 0.0 collective-permute-done.16.a_3_
  63.9 0.0 all-to-all-done.1.a_4_
  63.9 0.8 %shard_map.90 = (bf16[128,512]{1,0:T(8,128)(2,1)}, bf16[32,2048]{1,0:T(8,128)(2,1)}) custom-call(bf16[512,128]{1,0:T(8,128)(2,1)S(1)} %get-tuple-element.72.a_0_, bf16[512,128]{1,0:T(8,128)(2,1)S(1)} %collective-permute-done.14.a_1_, bf16[512,128]{1,0:T(8,128)(2,1)S(1)} %collective-permute-done.15.a_2_, bf16[512,128]{1,0:T(8,128)(2,1)S(1)} %collective-permute-done.16.a_3_, ...), custom_call_target="tpu_custom_call" | custom-call | tf_op jit(solution)/shard_map/pallas_call | solution.py:379
Async XLA Ops:
  0.6 19.8 %collective-permute-start.3 = (bf16[2,512,512]{2,1,0:T(8,128)(2,1)}, bf16[2,512,512]{2,1,0:T(8,128)(2,1)S(1)}, u32[]{:S(2)}, u32[]{:S(2)}) collective-permute-start(bf16[2,512,512]{2,1,0:T(8,128)(2,1)} %a_5_.1), channel_id=1, source_target_pairs={{0,16},{16,0},{1,17},{17,1},{2,18},{18,2},{3,19},{19,3},{4,20},{20... | collective-permute-start | bytes 3145736 | tf_op jit(solution)/shard_map/ppermute | solution.py:352
  1.1 19.3 %collective-permute-start.4 = (bf16[2,512,512]{2,1,0:T(8,128)(2,1)}, bf16[2,512,512]{2,1,0:T(8,128)(2,1)S(1)}, u32[]{:S(2)}, u32[]{:S(2)}) collective-permute-start(bf16[2,512,512]{2,1,0:T(8,128)(2,1)} %a_6_.1), channel_id=1, source_target_pairs={{0,16},{16,0},{1,17},{17,1},{2,18},{18,2},{3,19},{19,3},{4,20},{20... | collective-permute-start | bytes 3145736 | tf_op jit(solution)/shard_map/ppermute | solution.py:352
  2.7 13.0 %all-to-all-start = ((bf16[4,32,512]{2,1,0:T(8,128)(2,1)}), bf16[4,32,512]{2,1,0:T(8,128)(2,1)S(1)}, u32[]{:S(2)}, u32[]{:S(2)}) async-start(bf16[4,32,512]{2,1,0:T(8,128)(2,1)} %shard_map.85), calls=%async_computation | async-start | bytes 262144 | tf_op jit(solution)/shard_map/all_to_all | solution.py:375
  9.0 6.7 %collective-permute-start.1 = (bf16[128,512]{1,0:T(8,128)(2,1)}, bf16[128,512]{1,0:T(8,128)(2,1)S(1)}, u32[]{:S(2)}, u32[]{:S(2)}) collective-permute-start(bf16[128,512]{1,0:T(8,128)(2,1)} %a_1_.1), channel_id=1, source_target_pairs={{0,12},{4,8},{8,4},{12,0},{1,13},{5,9},{9,5},{13,1},{2,14},{6,10},... | collective-permute-start | bytes 393224 | tf_op jit(solution)/shard_map/ppermute | solution.py:352
  11.5 7.5 %collective-permute-start = (bf16[128,512]{1,0:T(8,128)(2,1)}, bf16[128,512]{1,0:T(8,128)(2,1)S(1)}, u32[]{:S(2)}, u32[]{:S(2)}) collective-permute-start(bf16[128,512]{1,0:T(8,128)(2,1)} %a_1_.1), channel_id=1, source_target_pairs={{0,8},{4,12},{8,0},{12,4},{1,9},{5,13},{9,1},{13,5},{2,10},{6,14},... | collective-permute-start | bytes 393224 | tf_op jit(solution)/shard_map/ppermute | solution.py:352
  12.0 8.0 %collective-permute-start.2 = (bf16[128,512]{1,0:T(8,128)(2,1)}, bf16[128,512]{1,0:T(8,128)(2,1)S(1)}, u32[]{:S(2)}, u32[]{:S(2)}) collective-permute-start(bf16[128,512]{1,0:T(8,128)(2,1)} %a_1_.1), channel_id=1, source_target_pairs={{0,4},{4,0},{8,12},{12,8},{1,5},{5,1},{9,13},{13,9},{2,6},{6,2},{1... | collective-permute-start | bytes 393224 | tf_op jit(solution)/shard_map/ppermute | solution.py:352
  15.7 13.4 %collective-permute-start.7 = (bf16[128,512]{1,0:T(8,128)(2,1)S(1)}, bf16[128,512]{1,0:T(8,128)(2,1)S(1)}, u32[]{:S(2)}, u32[]{:S(2)}) collective-permute-start(bf16[128,512]{1,0:T(8,128)(2,1)S(1)} %bitcast.4), channel_id=1, source_target_pairs={{0,12},{4,8},{8,4},{12,0},{1,13},{5,9},{9,5},{13,1},{2,14},{6,10},... | collective-permute-start | bytes 393224 | tf_op jit(solution)/shard_map/ppermute | solution.py:352
  19.0 10.1 %collective-permute-start.6 = (bf16[128,512]{1,0:T(8,128)(2,1)S(1)}, bf16[128,512]{1,0:T(8,128)(2,1)S(1)}, u32[]{:S(2)}, u32[]{:S(2)}) collective-permute-start(bf16[128,512]{1,0:T(8,128)(2,1)S(1)} %bitcast.5), channel_id=1, source_target_pairs={{0,8},{4,12},{8,0},{12,4},{1,9},{5,13},{9,1},{13,5},{2,10},{6,14},... | collective-permute-start | bytes 393224 | tf_op jit(solution)/shard_map/ppermute | solution.py:352
  20.0 9.1 %collective-permute-start.5 = (bf16[128,512]{1,0:T(8,128)(2,1)S(1)}, bf16[128,512]{1,0:T(8,128)(2,1)S(1)}, u32[]{:S(2)}, u32[]{:S(2)}) collective-permute-start(bf16[128,512]{1,0:T(8,128)(2,1)S(1)} %bitcast.6), channel_id=1, source_target_pairs={{0,4},{4,0},{8,12},{12,8},{1,5},{5,1},{9,13},{13,9},{2,6},{6,2},{1... | collective-permute-start | bytes 393224 | tf_op jit(solution)/shard_map/ppermute | solution.py:352
  30.1 6.1 %collective-permute-start.10 = (f32[4,4,512]{2,1,0:T(4,128)S(1)}, f32[4,4,512]{2,1,0:T(4,128)S(1)}, u32[]{:S(2)}, u32[]{:S(2)}) collective-permute-start(f32[4,4,512]{2,1,0:T(4,128)S(1)} %get-tuple-element.47.a_9_.a_5_), channel_id=1, source_target_pairs={{0,12},{4,8},{8,4},{12,0},{1,13},{5,9},{9,5},{13,1},{2,14},{6,10},... | collective-permute-start | bytes 98312 | tf_op jit(solution)/shard_map/ppermute | solution.py:352
  32.1 5.3 %collective-permute-start.9 = (f32[4,4,512]{2,1,0:T(4,128)S(1)}, f32[4,4,512]{2,1,0:T(4,128)S(1)}, u32[]{:S(2)}, u32[]{:S(2)}) collective-permute-start(f32[4,4,512]{2,1,0:T(4,128)S(1)} %get-tuple-element.47.a_9_.a_5_), channel_id=1, source_target_pairs={{0,8},{4,12},{8,0},{12,4},{1,9},{5,13},{9,1},{13,5},{2,10},{6,14},... | collective-permute-start | bytes 98312 | tf_op jit(solution)/shard_map/ppermute | solution.py:352
  33.1 4.3 %collective-permute-start.8 = (f32[4,4,512]{2,1,0:T(4,128)S(1)}, f32[4,4,512]{2,1,0:T(4,128)S(1)}, u32[]{:S(2)}, u32[]{:S(2)}) collective-permute-start(f32[4,4,512]{2,1,0:T(4,128)S(1)} %get-tuple-element.47.a_9_.a_5_), channel_id=1, source_target_pairs={{0,4},{4,0},{8,12},{12,8},{1,5},{5,1},{9,13},{13,9},{2,6},{6,2},{1... | collective-permute-start | bytes 98312 | tf_op jit(solution)/shard_map/ppermute | solution.py:352
  33.6 14.3 %collective-permute-start.11 = (bf16[512,128]{1,0:T(8,128)(2,1)S(1)}, bf16[512,128]{1,0:T(8,128)(2,1)S(1)}, u32[]{:S(2)}, u32[]{:S(2)}) collective-permute-start(bf16[512,128]{1,0:T(8,128)(2,1)S(1)} %get-tuple-element.60), channel_id=1, source_target_pairs={{0,4},{4,0},{8,12},{12,8},{1,5},{5,1},{9,13},{13,9},{2,6},{6,2},{1... | collective-permute-start | bytes 393224 | tf_op jit(solution)/shard_map/ppermute | solution.py:352
  35.2 12.7 %collective-permute-start.12 = (bf16[512,128]{1,0:T(8,128)(2,1)S(1)}, bf16[512,128]{1,0:T(8,128)(2,1)S(1)}, u32[]{:S(2)}, u32[]{:S(2)}) collective-permute-start(bf16[512,128]{1,0:T(8,128)(2,1)S(1)} %get-tuple-element.61), channel_id=1, source_target_pairs={{0,8},{4,12},{8,0},{12,4},{1,9},{5,13},{9,1},{13,5},{2,10},{6,14},... | collective-permute-start | bytes 393224 | tf_op jit(solution)/shard_map/ppermute | solution.py:352
  36.2 11.7 %collective-permute-start.13 = (bf16[512,128]{1,0:T(8,128)(2,1)S(1)}, bf16[512,128]{1,0:T(8,128)(2,1)S(1)}, u32[]{:S(2)}, u32[]{:S(2)}) collective-permute-start(bf16[512,128]{1,0:T(8,128)(2,1)S(1)} %get-tuple-element.62), channel_id=1, source_target_pairs={{0,12},{4,8},{8,4},{12,0},{1,13},{5,9},{9,5},{13,1},{2,14},{6,10},... | collective-permute-start | bytes 393224 | tf_op jit(solution)/shard_map/ppermute | solution.py:352
  47.9 9.8 %collective-permute-start.17 = (bf16[2,512,512]{2,1,0:T(8,128)(2,1)S(1)}, bf16[2,512,512]{2,1,0:T(8,128)(2,1)S(1)}, u32[]{:S(2)}, u32[]{:S(2)}) collective-permute-start(bf16[2,512,512]{2,1,0:T(8,128)(2,1)S(1)} %get-tuple-element.67), channel_id=1, source_target_pairs={{0,16},{16,0},{1,17},{17,1},{2,18},{18,2},{3,19},{19,3},{4,20},{20... | collective-permute-start | bytes 3145736 | tf_op jit(solution)/shard_map/ppermute | solution.py:352
  49.4 14.6 %all-to-all-start.1 = ((bf16[4,32,512]{2,1,0:T(8,128)(2,1)}), bf16[4,32,512]{2,1,0:T(8,128)(2,1)S(1)}, u32[]{:S(2)}, u32[]{:S(2)}) async-start(bf16[4,32,512]{2,1,0:T(8,128)(2,1)} %bitcast.3), calls=%async_computation.1 | async-start | bytes 262144 | tf_op jit(solution)/shard_map/all_to_all | solution.py:375
  54.2 5.8 %collective-permute-start.14 = (bf16[512,128]{1,0:T(8,128)(2,1)S(1)}, bf16[512,128]{1,0:T(8,128)(2,1)S(1)}, u32[]{:S(2)}, u32[]{:S(2)}) collective-permute-start(bf16[512,128]{1,0:T(8,128)(2,1)S(1)} %get-tuple-element.64), channel_id=1, source_target_pairs={{0,4},{4,0},{8,12},{12,8},{1,5},{5,1},{9,13},{13,9},{2,6},{6,2},{1... | collective-permute-start | bytes 393224 | tf_op jit(solution)/shard_map/ppermute | solution.py:352
  55.8 8.1 %collective-permute-start.15 = (bf16[512,128]{1,0:T(8,128)(2,1)S(1)}, bf16[512,128]{1,0:T(8,128)(2,1)S(1)}, u32[]{:S(2)}, u32[]{:S(2)}) collective-permute-start(bf16[512,128]{1,0:T(8,128)(2,1)S(1)} %get-tuple-element.65), channel_id=1, source_target_pairs={{0,8},{4,12},{8,0},{12,4},{1,9},{5,13},{9,1},{13,5},{2,10},{6,14},... | collective-permute-start | bytes 393224 | tf_op jit(solution)/shard_map/ppermute | solution.py:352
  56.7 7.3 %collective-permute-start.16 = (bf16[512,128]{1,0:T(8,128)(2,1)S(1)}, bf16[512,128]{1,0:T(8,128)(2,1)S(1)}, u32[]{:S(2)}, u32[]{:S(2)}) collective-permute-start(bf16[512,128]{1,0:T(8,128)(2,1)S(1)} %get-tuple-element.66), channel_id=1, source_target_pairs={{0,12},{4,8},{8,4},{12,0},{1,13},{5,9},{9,5},{13,1},{2,14},{6,10},... | collective-permute-start | bytes 393224 | tf_op jit(solution)/shard_map/ppermute | solution.py:352
